TPU v7x, 32 devices: a whole 2x2x4 slice. The times are simulated.
32 devices in a mesh: replica: 2 (over x), shard: 4 (over z), seq: 4 (over y, core).
Axes of the slice: x: 2, y: 2, z: 4, core: 2. Of those that a mesh axis runs over, the one named last changes fastest.
Arguments:
- activations: bfloat16 [8, 2, 1024, 1024], P(('replica', 'shard'), None, 'seq'), may hold values from -6 to 6
- cotangent: bfloat16 [8, 2, 1024, 1024], P(('replica', 'shard'), None, 'seq'), may hold values from -6 to 6
- clip_loads: int32 [8], P(('replica', 'shard')), may hold values from 1 to 2, as said below
- attn_gain: bfloat16 [1024], P('shard'), may hold values from 0.5 to 1.5
- attn_shift: bfloat16 [1024], P('shard'), may hold values from -1.5 to 1.5
- w_qkv: bfloat16 [1024, 3072], P('shard'), may hold values from -0.1875 to 0.1875
- q_bias: bfloat16 [1024], P('shard'), may hold values from -1.5 to 1.5
- v_bias: bfloat16 [1024], P('shard'), may hold values from -1.5 to 1.5
- w_out: bfloat16 [1024, 1024], P('shard'), may hold values from -0.75 to 0.75
- out_bias: bfloat16 [1024], P('shard'), may hold values from -1.5 to 1.5
- mlp_gain: bfloat16 [1024], P('shard'), may hold values from 0.5 to 1.5
- mlp_shift: bfloat16 [1024], P('shard'), may hold values from -1.5 to 1.5
- w_up: bfloat16 [1024, 4096], P('shard'), may hold values from -0.1875 to 0.1875
- up_bias: bfloat16 [4096], P('shard'), may hold values from -1.5 to 1.5
- w_down: bfloat16 [4096, 1024], P('shard'), may hold values from -0.09375 to 0.09375
- down_bias: bfloat16 [1024], P('shard'), may hold values from -1.5 to 1.5
Outputs:
- layer_out: bfloat16 [8, 2, 1024, 1024], P(('replica', 'shard'), None, 'seq')
- input_grad: bfloat16 [8, 2, 1024, 1024], P(('replica', 'shard'), None, 'seq')
- grad_attn_gain: float32 [1024], P(('shard', 'seq'))
- grad_attn_shift: float32 [1024], P(('shard', 'seq'))
- grad_w_qkv: float32 [1024, 3072], P(('shard', 'seq'))
- grad_q_bias: float32 [1024], P(('shard', 'seq'))
- grad_v_bias: float32 [1024], P(('shard', 'seq'))
- grad_w_out: float32 [1024, 1024], P(('shard', 'seq'))
- grad_out_bias: float32 [1024], P(('shard', 'seq'))
- grad_mlp_gain: float32 [1024], P(('shard', 'seq'))
- grad_mlp_shift: float32 [1024], P(('shard', 'seq'))
- grad_w_up: float32 [1024, 4096], P(('shard', 'seq'))
- grad_up_bias: float32 [4096], P(('shard', 'seq'))
- grad_w_down: float32 [4096, 1024], P(('shard', 'seq'))
- grad_down_bias: float32 [1024], P(('shard', 'seq'))
Inputs may be any that keep to these rules, and one draw needn't show every extreme that they name: Group g holds live clips in its first clip_loads[g] of 2 slots; the remaining slots are empty.
All inputs are finite; a program needn't handle non-finite values.
Results may differ from a plain program's by a relative error of at most 0.014.
Values may be sent and summed in bfloat16 or wider, within the bound.
A program may use at most 256 MiB of HBM per device.

v0:
```python
import jax
import jax.numpy as jnp
from jax import lax
from jax.sharding import PartitionSpec as P

HEADS = 16
HEAD_DIM = 64


EPSILON = 1e-06


def layer_norm(values, gain, shift):
    center = values - jnp.mean(values, axis=-1, keepdims=True)
    spread = jnp.mean(center * center, axis=-1, keepdims=True)
    return center * lax.rsqrt(spread + EPSILON) * gain + shift


def norm_pull(values, gain, shift, incoming):
    _, pull = jax.vjp(layer_norm, values, gain, shift)
    return pull(incoming)


def gelu_exact(values):
    return jax.nn.gelu(values, approximate=False)


def contract_rows(left, right):
    return lax.dot_general(
        left, right, (((0,), (0,)), ((), ())), preferred_element_type=jnp.float32
    )


def contract_cols(left, right):
    return lax.dot_general(
        left, right, (((1,), (1,)), ((), ())), preferred_element_type=jnp.float32
    )


def attention_scores(queries, key_heads):
    return jnp.einsum(
        "thd,lhd->htl", queries, key_heads, preferred_element_type=jnp.float32
    ) * HEAD_DIM ** (-0.5)


def row_total(values):
    return jnp.sum(values.astype(jnp.float32), axis=0)


def forward(gathered, inputs):
    (
        attn_gain,
        attn_shift,
        w_qkv,
        q_bias,
        v_bias,
        w_out,
        out_bias,
        mlp_gain,
        mlp_shift,
        w_up,
        up_bias,
        w_down,
        down_bias,
    ) = gathered
    length, width = inputs.shape
    normed = layer_norm(
        inputs, attn_gain.astype(jnp.float32), attn_shift.astype(jnp.float32)
    ).astype(jnp.bfloat16)
    bias_row = jnp.concatenate([q_bias, jnp.zeros_like(q_bias), v_bias]).astype(jnp.float32)
    project = (jnp.dot(normed, w_qkv, preferred_element_type=jnp.float32) + bias_row).astype(
        jnp.bfloat16
    )
    key_rows, value_rows = (
        lax.all_gather(project[:, width : 2 * width], "seq", axis=0, tiled=True),
        lax.all_gather(project[:, 2 * width :], "seq", axis=0, tiled=True),
    )
    queries = project[:, :width].reshape(length, HEADS, HEAD_DIM)
    key_heads = key_rows.reshape(-1, HEADS, HEAD_DIM)
    value_heads = value_rows.reshape(-1, HEADS, HEAD_DIM)
    scores = attention_scores(queries, key_heads)
    highest = jnp.max(scores, axis=-1, keepdims=True)
    expo_terms = jnp.exp(scores - highest)
    totals = jnp.sum(expo_terms, axis=-1, keepdims=True)
    softmax_low = (expo_terms / totals).astype(jnp.bfloat16)
    log_total = highest + jnp.log(totals)
    attended = jnp.einsum(
        "htl,lhd->thd", softmax_low, value_heads, preferred_element_type=jnp.float32
    )
    attended = attended.reshape(length, width).astype(jnp.bfloat16)
    residual = (
        inputs
        + jnp.dot(attended, w_out, preferred_element_type=jnp.float32)
        + out_bias.astype(jnp.float32)
    )
    normed_mlp = layer_norm(
        residual, mlp_gain.astype(jnp.float32), mlp_shift.astype(jnp.float32)
    ).astype(jnp.bfloat16)
    pre_act = jnp.dot(normed_mlp, w_up, preferred_element_type=jnp.float32) + up_bias.astype(
        jnp.float32
    )
    activated = gelu_exact(pre_act).astype(jnp.bfloat16)
    layer_out = (
        residual
        + jnp.dot(activated, w_down, preferred_element_type=jnp.float32)
        + down_bias.astype(jnp.float32)
    )
    kept = (
        normed,
        project,
        key_heads,
        value_heads,
        log_total,
        attended,
        residual,
        normed_mlp,
        pre_act,
        activated,
    )
    return (layer_out, kept)


def backward(gathered, inputs, kept, out_grad):
    (
        attn_gain,
        attn_shift,
        w_qkv,
        q_bias,
        v_bias,
        w_out,
        out_bias,
        mlp_gain,
        mlp_shift,
        w_up,
        up_bias,
        w_down,
        down_bias,
    ) = gathered
    (
        normed,
        project,
        key_heads,
        value_heads,
        log_total,
        attended,
        residual,
        normed_mlp,
        pre_act,
        activated,
    ) = kept
    length, width = inputs.shape
    score_scale = HEAD_DIM ** (-0.5)
    d_mlp = out_grad.astype(jnp.bfloat16)
    grad_w_down = contract_rows(activated, d_mlp)
    grad_down_bias = row_total(d_mlp)
    d_act = contract_cols(d_mlp, w_down)
    _, gelu_pull = jax.vjp(gelu_exact, pre_act)
    d_pre = gelu_pull(d_act)[0].astype(jnp.bfloat16)
    grad_w_up = contract_rows(normed_mlp, d_pre)
    grad_up_bias = row_total(d_pre)
    d_norm = contract_cols(d_pre, w_up)
    d_res_norm, grad_mlp_gain, grad_mlp_shift = norm_pull(
        residual, mlp_gain.astype(jnp.float32), mlp_shift.astype(jnp.float32), d_norm
    )
    d_residual = out_grad + d_res_norm
    d_branch = d_residual.astype(jnp.bfloat16)
    grad_w_out = contract_rows(attended, d_branch)
    grad_out_bias = row_total(d_branch)
    d_attended = (
        contract_cols(d_branch, w_out).astype(jnp.bfloat16).reshape(length, HEADS, HEAD_DIM)
    )
    queries = project[:, :width].reshape(length, HEADS, HEAD_DIM)
    scores = attention_scores(queries, key_heads)
    probs_full = jnp.exp(scores - log_total)
    softmax_low = probs_full.astype(jnp.bfloat16)
    d_probs = jnp.einsum(
        "thd,lhd->htl", d_attended, value_heads, preferred_element_type=jnp.float32
    )
    d_scores = probs_full * (d_probs - jnp.sum(probs_full * d_probs, axis=-1, keepdims=True))
    d_scores = d_scores.astype(jnp.bfloat16)
    d_query = (
        jnp.einsum("htl,lhd->thd", d_scores, key_heads, preferred_element_type=jnp.float32)
        * score_scale
    )
    d_query = d_query.reshape(length, width).astype(jnp.bfloat16)
    count = lax.axis_size("seq") * length
    d_key = (
        jnp.einsum("htl,thd->lhd", d_scores, queries, preferred_element_type=jnp.float32)
        * score_scale
    )
    d_value = jnp.einsum(
        "htl,thd->lhd", softmax_low, d_attended, preferred_element_type=jnp.float32
    )
    key_grads = lax.psum_scatter(
        jnp.concatenate(
            [d_key.reshape(count, width), d_value.reshape(count, width)], axis=1
        ).astype(jnp.bfloat16),
        "seq",
        scatter_dimension=0,
        tiled=True,
    )
    d_project = jnp.concatenate([d_query, key_grads], axis=1)
    grad_w_qkv = contract_rows(normed, d_project)
    grad_q_bias = row_total(d_query)
    grad_v_bias = row_total(key_grads[:, width:])
    d_norm_first = contract_cols(d_project, w_qkv)
    d_in_norm, grad_attn_gain, grad_attn_shift = norm_pull(
        inputs, attn_gain.astype(jnp.float32), attn_shift.astype(jnp.float32), d_norm_first
    )
    input_grad = d_residual + d_in_norm
    gradients = (
        grad_attn_gain,
        grad_attn_shift,
        grad_w_qkv,
        grad_q_bias,
        grad_v_bias,
        grad_w_out,
        grad_out_bias,
        grad_mlp_gain,
        grad_mlp_shift,
        grad_w_up,
        grad_up_bias,
        grad_w_down,
        grad_down_bias,
    )
    return (input_grad, gradients)


def local(
    activations,
    cotangent,
    clip_loads,
    attn_gain,
    attn_shift,
    w_qkv,
    q_bias,
    v_bias,
    w_out,
    out_bias,
    mlp_gain,
    mlp_shift,
    w_up,
    up_bias,
    w_down,
    down_bias,
):
    gathered = (
        lax.all_gather(attn_gain, "shard", axis=0, tiled=True),
        lax.all_gather(attn_shift, "shard", axis=0, tiled=True),
        lax.all_gather(w_qkv, "shard", axis=0, tiled=True),
        lax.all_gather(q_bias, "shard", axis=0, tiled=True),
        lax.all_gather(v_bias, "shard", axis=0, tiled=True),
        lax.all_gather(w_out, "shard", axis=0, tiled=True),
        lax.all_gather(out_bias, "shard", axis=0, tiled=True),
        lax.all_gather(mlp_gain, "shard", axis=0, tiled=True),
        lax.all_gather(mlp_shift, "shard", axis=0, tiled=True),
        lax.all_gather(w_up, "shard", axis=0, tiled=True),
        lax.all_gather(up_bias, "shard", axis=0, tiled=True),
        lax.all_gather(w_down, "shard", axis=0, tiled=True),
        lax.all_gather(down_bias, "shard", axis=0, tiled=True),
    )
    slot_count = activations.shape[1]
    live_count = clip_loads[0]
    output_rows = []
    input_rows = []
    summed = None
    for slot_index in range(slot_count):
        inputs = activations[0, slot_index].astype(jnp.float32)
        live_weight = (slot_index < live_count).astype(jnp.float32)
        out_grad = cotangent[0, slot_index].astype(jnp.float32) * live_weight
        layer_out, kept = forward(gathered, inputs)
        input_grad, gradients = backward(gathered, inputs, kept, out_grad)
        layer_out = layer_out * live_weight
        output_rows.append(layer_out.astype(jnp.bfloat16))
        input_rows.append(input_grad.astype(jnp.bfloat16))
        if slot_index == 0:
            summed = tuple(gradients)
        else:
            summed = tuple(jax.tree.map(jnp.add, summed, tuple(gradients)))
    summed = (
        lax.psum_scatter(summed[0], ("shard", "seq"), scatter_dimension=0, tiled=True),
        lax.psum_scatter(summed[1], ("shard", "seq"), scatter_dimension=0, tiled=True),
        lax.psum_scatter(summed[2], ("shard", "seq"), scatter_dimension=0, tiled=True),
        lax.psum_scatter(summed[3], ("shard", "seq"), scatter_dimension=0, tiled=True),
        lax.psum_scatter(summed[4], ("shard", "seq"), scatter_dimension=0, tiled=True),
        lax.psum_scatter(summed[5], ("shard", "seq"), scatter_dimension=0, tiled=True),
        lax.psum_scatter(summed[6], ("shard", "seq"), scatter_dimension=0, tiled=True),
        lax.psum_scatter(summed[7], ("shard", "seq"), scatter_dimension=0, tiled=True),
        lax.psum_scatter(summed[8], ("shard", "seq"), scatter_dimension=0, tiled=True),
        lax.psum_scatter(summed[9], ("shard", "seq"), scatter_dimension=0, tiled=True),
        lax.psum_scatter(summed[10], ("shard", "seq"), scatter_dimension=0, tiled=True),
        lax.psum_scatter(summed[11], ("shard", "seq"), scatter_dimension=0, tiled=True),
        lax.psum_scatter(summed[12], ("shard", "seq"), scatter_dimension=0, tiled=True),
    )
    totals = (
        lax.psum(summed[0].astype(jnp.bfloat16), "replica").astype(jnp.float32),
        lax.psum(summed[1].astype(jnp.bfloat16), "replica").astype(jnp.float32),
        lax.psum(summed[2].astype(jnp.bfloat16), "replica").astype(jnp.float32),
        lax.psum(summed[3].astype(jnp.bfloat16), "replica").astype(jnp.float32),
        lax.psum(summed[4].astype(jnp.bfloat16), "replica").astype(jnp.float32),
        lax.psum(summed[5].astype(jnp.bfloat16), "replica").astype(jnp.float32),
        lax.psum(summed[6].astype(jnp.bfloat16), "replica").astype(jnp.float32),
        lax.psum(summed[7].astype(jnp.bfloat16), "replica").astype(jnp.float32),
        lax.psum(summed[8].astype(jnp.bfloat16), "replica").astype(jnp.float32),
        lax.psum(summed[9].astype(jnp.bfloat16), "replica").astype(jnp.float32),
        lax.psum(summed[10].astype(jnp.bfloat16), "replica").astype(jnp.float32),
        lax.psum(summed[11].astype(jnp.bfloat16), "replica").astype(jnp.float32),
        lax.psum(summed[12].astype(jnp.bfloat16), "replica").astype(jnp.float32),
    )
    layer_out = jnp.stack(output_rows)[None]
    input_grad = jnp.stack(input_rows)[None]
    return (
        layer_out,
        input_grad,
        totals[0],
        totals[1],
        totals[2],
        totals[3],
        totals[4],
        totals[5],
        totals[6],
        totals[7],
        totals[8],
        totals[9],
        totals[10],
        totals[11],
        totals[12],
    )


def solution(mesh):
    placed = (
        P(("replica", "shard"), None, "seq", None),
        P(("replica", "shard"), None, "seq", None),
        P(("replica", "shard")),
        P("shard"),
        P("shard"),
        P("shard", None),
        P("shard"),
        P("shard"),
        P("shard", None),
        P("shard"),
        P("shard"),
        P("shard"),
        P("shard", None),
        P("shard"),
        P("shard", None),
        P("shard"),
    )
    return jax.shard_map(
        local,
        mesh=mesh,
        in_specs=placed,
        out_specs=(
            P(("replica", "shard"), None, "seq", None),
            P(("replica", "shard"), None, "seq", None),
            P(("shard", "seq")),
            P(("shard", "seq")),
            P(("shard", "seq"), None),
            P(("shard", "seq")),
            P(("shard", "seq")),
            P(("shard", "seq"), None),
            P(("shard", "seq")),
            P(("shard", "seq")),
            P(("shard", "seq")),
            P(("shard", "seq"), None),
            P(("shard", "seq")),
            P(("shard", "seq"), None),
            P(("shard", "seq")),
        ),
        check_vma=False,
    )
```

profile of v0, /device:TPU:0, one launch (start us, length us, event | category | flops | bytes accessed | tf_op | source)
XLA Modules:
  0.0 1416.9 jit_solution(11576040717675768584)
XLA Ops:
  8.6 12.6 all-gather.3
  30.3 14.4 %all-gather.1 = bf16[4,1,256]{2,1,0:T(2,128)(2,1)S(1)} all-gather(bf16[1,1,256]{2,1,0:T(2,128)(2,1)S(1)} %reshape.283), channel_id=1, replica_groups=mesh['replica'=2,'shard'=4,'seq'=4] {'shard'}, dimensions={0}, use_global_device_ids=true | all-gather | bytes 2560 | tf_op jit(solution)/shard_map/all_gather | solution.py:249
  56.3 71.5 %all-gather.17.cloned.1.call-done = bf16[1024,3072]{1,0:T(8,128)(2,1)} async-done(((bf16[256,3072]{1,0:T(8,128)(2,1)}), bf16[1024,3072]{1,0:T(8,128)(2,1)}) %all-gather.17.cloned.1.call-update) | async-done | bytes 6291472 | tf_op jit(solution)/shard_map/all_gather | solution.py:250
  151.2 11.9 all_gather.63
  172.1 9.3 all-gather.5
  203.2 9.1 fusion.54
  216.4 12.4 all-gather.21.cloned.1.call-done
  232.8 43.4 %all-gather.23.cloned.1.call-done = bf16[1024,1024]{1,0:T(8,128)(2,1)} async-done(((bf16[256,1024]{1,0:T(8,128)(2,1)}), bf16[1024,1024]{1,0:T(8,128)(2,1)}) %all-gather.23.cloned.1.call-update) | async-done | bytes 2097168 | tf_op jit(solution)/shard_map/all_gather | solution.py:253
  296.1 130.1 %all-gather.25.cloned.1.call-done = bf16[1024,4096]{1,0:T(8,128)(2,1)} async-done(((bf16[256,4096]{1,0:T(8,128)(2,1)}), bf16[1024,4096]{1,0:T(8,128)(2,1)}) %all-gather.25.cloned.1.call-update) | async-done | bytes 8388624 | tf_op jit(solution)/shard_map/all_gather | solution.py:257
  426.2 16.2 %multiply_convert_fusion.4 = (bf16[256,4096]{1,0:T(8,128)(2,1)}, f32[256,4096]{1,0:T(8,128)}, f32[256,4096]{1,0:T(8,128)}) fusion(f32[4096]{0:T(1024)S(1)} %copy-done.76, bf16[1024,4096]{1,0:T(8,128)(2,1)} %all-gather.25.cloned.1.call-done, f32[256,1024]{1,0:T(8,128)S(1)} %get-tuple-element.89, f32[256]{0:T(256)S(1)} %fusion.85, ...), kind=kOutput, calls=%fused_computation.41 | convolution fusion | flops 2218000384 | bytes 19949568 | tf_op jit(solution)/shard_map/dot_general | solution.py:99
  442.4 16.5 %multiply_convert_fusion.5 = (bf16[256,4096]{1,0:T(8,128)(2,1)}, f32[256,4096]{1,0:T(8,128)}, f32[256,4096]{1,0:T(8,128)}) fusion(f32[4096]{0:T(1024)S(1)} %copy-done.76, bf16[1024,4096]{1,0:T(8,128)(2,1)S(1)} %copy-done.98, f32[256,1024]{1,0:T(8,128)S(1)} %get-tuple-element.94, f32[1024]{0:T(1024)S(1)} %bitcast.264, f32[1024]{0:T(1024)S(1)} %bitcast.250, ...), kind=kOutput, calls=%fused_computation.54 | convolution fusion | flops 2218000384 | bytes 19949568 | tf_op jit(solution)/shard_map/dot_general | solution.py:99
  458.9 116.8 %all-gather.27.cloned.1.call-done = bf16[4096,1024]{1,0:T(8,128)(2,1)} async-done(((bf16[1024,1024]{1,0:T(8,128)(2,1)}), bf16[4096,1024]{1,0:T(8,128)(2,1)}) %all-gather.27.cloned.1.call-update) | async-done | bytes 8388624 | tf_op jit(solution)/shard_map/all_gather | solution.py:259
  575.6 12.2 convert_reduce_fusion
  613.9 9.8 fusion.28
  623.7 14.1 multiply_reduce_fusion.1
  659.1 16.4 %multiply_reduce_fusion = (f32[16,256]{1,0:T(8,128)}, f32[16,256,1024]{2,1,0:T(8,128)}) fusion(f32[16,256,1024]{2,1,0:T(8,128)} %copy-done, f32[16,256]{1,0:T(8,128)} %log_add_fusion, bf16[256,16,64]{0,2,1:T(8,128)(2,1)} %bitcast.237, bf16[1024,16,64]{0,2,1:T(8,128)(2,1)} %bitcast.228), kind=kOutput, calls=%fused_computation.1 | convolution fusion | flops 553644032 | bytes 36208640 | tf_op jit(solution)/shard_map/thd,lhd->htl/dot_general | solution.py:176
  706.9 10.6 convolution_add_fusion.1
  722.7 9.9 convolution_add_fusion
  756.0 12.2 convolution_add_fusion.2
  797.2 21.6 %reduce-scatter.13.cloned.1.call-done = f32[64,1024]{1,0:T(8,128)} async-done(((f32[1024,1024]{1,0:T(8,128)}), f32[64,1024]{1,0:T(8,128)}) %reduce-scatter.13.cloned.1.call-update) | async-done | bytes 262160 | tf_op jit(solution)/shard_map/reduce_scatter | solution.py:286
  832.3 168.6 %reduce-scatter.15.cloned.1.call-done = f32[64,4096]{1,0:T(8,128)} async-done(((f32[1024,4096]{1,0:T(8,128)}), f32[64,4096]{1,0:T(8,128)}) %reduce-scatter.15.cloned.1.call-update) | async-done | bytes 1048592 | tf_op jit(solution)/shard_map/reduce_scatter | solution.py:290
  1003.0 180.1 %reduce-scatter.17.cloned.1.call-done = f32[256,1024]{1,0:T(8,128)} async-done(((f32[4096,1024]{1,0:T(8,128)}), f32[256,1024]{1,0:T(8,128)}) %reduce-scatter.17.cloned.1.call-update) | async-done | bytes 1048592 | tf_op jit(solution)/shard_map/reduce_scatter | solution.py:292
  1185.3 136.1 %reduce-scatter.11.cloned.1.call-done = f32[64,3072]{1,0:T(8,128)} async-done(((f32[1024,3072]{1,0:T(8,128)}), f32[64,3072]{1,0:T(8,128)}) %reduce-scatter.11.cloned.1.call-update) | async-done | bytes 786448 | tf_op jit(solution)/shard_map/reduce_scatter | solution.py:283
  1328.6 59.8 %all-reduce.9 = (bf16[1024]{0:T(1024)(128)(2,1)S(1)}, bf16[1024]{0:T(1024)(128)(2,1)S(1)}, bf16[1024]{0:T(1024)(128)(2,1)S(1)}, bf16[1024]{0:T(1024)(128)(2,1)S(...) all-reduce(f32[1024]{0:T(1024)S(1)} %add.298, ...), channel_id=4, replica_groups=mesh['replica'=2,'shard'=4,'seq'=4] {'shard','seq'}, use_global_device_ids=true, to_apply=%region_26.0.clone | all-reduce | flops 12288 | bytes 73728
  (398 shorter events, 283.9 us)
Async XLA Ops:
  7.2 120.6 %all-gather.17.cloned.1.call-start = ((), (), s32[]{:S(2)}) async-start(), calls=%async_computation.6 | async-start | bytes 7864320 | tf_op jit(solution)/shard_map/all_gather | solution.py:250
  7.9 176.1 %all-gather.31.cloned.1.call-start = ((), (), s32[]{:S(2)}) async-start(), calls=%async_computation.13 | async-start | bytes 2621440 | tf_op jit(solution)/shard_map/all_gather | solution.py:75
  133.8 66.4 %all-gather.29.cloned.1.call-start = ((), (), s32[]{:S(2)}) async-start(), calls=%async_computation.12 | async-start | bytes 2621440 | tf_op jit(solution)/shard_map/all_gather | solution.py:76
  134.6 77.8 %all-gather.19.cloned.1.call-start = ((), (), s32[]{:S(2)}) async-start(), calls=%async_computation.7 | async-start | bytes 2621440 | tf_op jit(solution)/shard_map/all_gather | solution.py:76
  140.6 88.2 %all-gather.21.cloned.1.call-start = ((), (), s32[]{:S(2)}) async-start(), calls=%async_computation.8 | async-start | bytes 2621440 | tf_op jit(solution)/shard_map/all_gather | solution.py:75
  141.2 135.0 %all-gather.23.cloned.1.call-start = ((), (), s32[]{:S(2)}) async-start(), calls=%async_computation.9 | async-start | bytes 2621440 | tf_op jit(solution)/shard_map/all_gather | solution.py:253
  141.8 284.4 %all-gather.25.cloned.1.call-start = ((), (), s32[]{:S(2)}) async-start(), calls=%async_computation.10 | async-start | bytes 10485760 | tf_op jit(solution)/shard_map/all_gather | solution.py:257
  142.5 433.1 %all-gather.27.cloned.1.call-start = ((), (), s32[]{:S(2)}) async-start(), calls=%async_computation.11 | async-start | bytes 10485760 | tf_op jit(solution)/shard_map/all_gather | solution.py:259
  143.3 604.4 %reduce-scatter.7.cloned.1.call-start = ((), (), s32[]{:S(2)}) async-start(), calls=%async_computation.14 | async-start | bytes 5242880 | tf_op jit(solution)/shard_map/reduce_scatter | solution.py:194
  278.8 330.4 %copy-start.62 = (f32[256]{0:T(256)}, f32[256]{0:T(256)S(1)}, u32[]{:S(2)}) copy-start(f32[256]{0:T(256)S(1)} %broadcast_multiply_fusion) | copy-start | bytes 3076
  652.2 103.8 %reduce-scatter.9.cloned.1.call-start = ((), (), s32[]{:S(2)}) async-start(), calls=%async_computation.15 | async-start | bytes 5242880 | tf_op jit(solution)/shard_map/reduce_scatter | solution.py:194
  696.8 122.0 %reduce-scatter.13.cloned.1.call-start = ((), (), s32[]{:S(2)}) async-start(), calls=%async_computation.17 | async-start | bytes 4456448 | tf_op jit(solution)/shard_map/reduce_scatter | solution.py:286
  701.5 299.4 %reduce-scatter.15.cloned.1.call-start = ((), (), s32[]{:S(2)}) async-start(), calls=%async_computation.18 | async-start | bytes 17825792 | tf_op jit(solution)/shard_map/reduce_scatter | solution.py:290
  717.6 465.6 %reduce-scatter.17.cloned.1.call-start = ((), (), s32[]{:S(2)}) async-start(), calls=%async_computation.19 | async-start | bytes 17825792 | tf_op jit(solution)/shard_map/reduce_scatter | solution.py:292
  732.7 588.7 %reduce-scatter.11.cloned.1.call-start = ((), (), s32[]{:S(2)}) async-start(), calls=%async_computation.16 | async-start | bytes 13369344 | tf_op jit(solution)/shard_map/reduce_scatter | solution.py:283
  768.3 634.2 %all-reduce.14.cloned.1.call-start = ((), (), s32[]{:S(2)}) async-start(), calls=%async_computation.20 | async-start | bytes 3145728 | tf_op jit(solution)/shard_map/psum | solution.py:298
  832.3 491.1 %copy-start.61 = (f32[256]{0:T(256)S(1)}, f32[256]{0:T(256)}, u32[]{:S(2)}) copy-start(f32[256]{0:T(256)} %copy-done.59) | copy-start | bytes 3076
  832.3 491.1 %copy-start.68 = (f32[256]{0:T(256)S(1)}, f32[256]{0:T(256)}, u32[]{:S(2)}) copy-start(f32[256]{0:T(256)} %copy-done.66) | copy-start | bytes 3076
  1003.0 325.6 %copy-start.72 = (f32[1024]{0:T(1024)S(1)}, f32[1024]{0:T(1024)}, u32[]{:S(2)}) copy-start(f32[1024]{0:T(1024)} %add.305) | copy-start | bytes 12292
  1003.0 325.6 %copy-start.73 = (f32[1024]{0:T(1024)S(1)}, f32[1024]{0:T(1024)}, u32[]{:S(2)}) copy-start(f32[1024]{0:T(1024)} %add.306) | copy-start | bytes 12292
  1003.0 325.6 %copy-start.74 = (f32[1024]{0:T(1024)S(1)}, f32[1024]{0:T(1024)}, u32[]{:S(2)}) copy-start(f32[1024]{0:T(1024)} %add.307) | copy-start | bytes 12292
  1003.0 325.6 %copy-start.75 = (f32[1024]{0:T(1024)S(1)}, f32[1024]{0:T(1024)}, u32[]{:S(2)}) copy-start(f32[1024]{0:T(1024)} %add.311) | copy-start | bytes 12292
  1003.0 395.7 %copy-start.15 = (bf16[1,2,256,1024]{3,2,1,0:T(8,128)(2,1)S(1)}, bf16[1,2,256,1024]{3,2,1,0:T(8,128)(2,1)}, u32[]{:S(2)}) copy-start(bf16[1,2,256,1024]{3,2,1,0:T(8,128)(2,1)} %param.17) | copy-start | bytes 3145732
  1003.0 395.7 %copy-start.86 = (f32[256]{0:T(256)S(1)}, f32[256]{0:T(256)}, u32[]{:S(2)}) copy-start(f32[256]{0:T(256)} %copy-done.85) | copy-start | bytes 3076
  (103 other events, 3699.0 us)
Sparse Core Ops, SparseCore 0:
  9.6 118.1 all-gather.16
  134.0 20.8 all-gather.30
  157.0 22.5 all-gather.28
  181.6 22.5 all-gather.18
  206.2 22.5 all-gather.20
  230.2 45.9 all-gather.22
  277.8 148.3 all-gather.24
  427.7 147.8 all-gather.26
  652.3 42.7 reduce-scatter.6
  697.6 44.5 reduce-scatter.8
  746.0 72.6 reduce-scatter.12
  823.3 177.6 reduce-scatter.14
  1005.6 177.5 reduce-scatter.16
  1187.6 133.7 reduce-scatter.10
  1324.4 51.1 all-reduce.13
where the time goes:
time: 1420 us
  waiting for transfers between devices  885 us (62%)
  matrix products  244 us (17%)
  blocking collectives  154 us (11%)
  other arithmetic  69 us (5%)
  local copies, waits for them, and re-layouts  47.3 us (3%)
  between operations  17.5 us (1%)
    reduce_scatter x1, waiting for transfers between devices, local(): lax.psum_scatter(summed[11], ('shard', 'seq'), scatter_dimension=0, tiled...  180 us
    reduce_scatter x1, waiting for transfers between devices, local(): lax.psum_scatter(summed[9], ('shard', 'seq'), scatter_dimension=0, tiled=...  169 us
    reduce_scatter x1, waiting for transfers between devices, local(): lax.psum_scatter(summed[2], ('shard', 'seq'), scatter_dimension=0, tiled=...  136 us
    all_gather x1, waiting for transfers between devices, local(): lax.all_gather(w_up, 'shard', axis=0, tiled=True)  130 us
    all_gather x1, waiting for transfers between devices, local(): lax.all_gather(w_down, 'shard', axis=0, tiled=True)  117 us
    all_gather x1, waiting for transfers between devices, local(): lax.all_gather(w_qkv, 'shard', axis=0, tiled=True)  71.5 us
    unnamed x1, blocking collectives  59.8 us
    dot_general x8, matrix products, contract_rows(): lax.dot_general(left, right, (((0,), (0,)), ((), ())), preferred_element_...  52.6 us
  transfers between devices with their start and end apart: 15, of which 9 were waited for; matrix products, arithmetic and copies ran while one was open for 17% of the time, Pallas kernels for 0%

commit v1 on v0

v1 whole, which is shorter than its diff:
```python
import functools

import jax
import jax.numpy as jnp
from jax import lax
from jax.experimental import pallas as pl
from jax.experimental.pallas import tpu as pltpu
from jax.sharding import PartitionSpec as P

MESH = pl.DeviceIdType.MESH
BF = jnp.bfloat16
F32 = jnp.float32
HEAD_DIM = 64
PAIR = 2 * HEAD_DIM
EPSILON = 1e-06
NN = (((1,), (0,)), ((), ()))
NT = (((1,), (1,)), ((), ()))
TN = (((0,), (0,)), ((), ()))
MIB = 2**20


def dot(a, b, dims=NN):
    return lax.dot_general(a, b, dims, preferred_element_type=F32)


class Place:
    def __init__(self, shards):
        self.shards = shards
        r, self.z, q = (lax.axis_index(a) for a in ("replica", "shard", "seq"))
        self.x, self.y, self.c = r % 2, q // 2, q % 2
        self.q = q
        self.to_x = {"replica": r + 1 - 2 * self.x}
        self.to_y = {"seq": q + 2 - 4 * self.y}
        self.to_c = {"seq": q + 1 - 2 * self.c}

    def to_z(self, shift):
        return {"shard": (self.z + shift) % self.shards}

    def behind(self, shift):
        return (self.z + self.shards - shift) % self.shards

    def greet(self):
        barrier = pltpu.get_barrier_semaphore()
        peers = [self.to_x, self.to_y, self.to_c]
        peers += [self.to_z(shift) for shift in range(1, self.shards)]
        for peer in peers:
            pl.semaphore_signal(barrier, inc=1, device_id=peer, device_id_type=MESH)
        pl.semaphore_wait(barrier, len(peers))


class Copies:
    def __init__(self, send_sems, recv_sems, local_sems):
        self.send_sems, self.recv_sems, self.local_sems = send_sems, recv_sems, local_sems
        self.remote, self.local = [], []

    def send(self, src, dst, peer):
        at = len(self.remote)
        copy = pltpu.make_async_remote_copy(
            src_ref=src, dst_ref=dst, send_sem=self.send_sems.at[at], recv_sem=self.recv_sems.at[at],
            device_id=peer, device_id_type=MESH,
        )
        copy.start()
        self.remote.append(copy)
        return copy

    def move(self, src, dst):
        at = len(self.local)
        copy = pltpu.make_async_copy(src, dst, self.local_sems.at[at])
        copy.start()
        self.local.append([copy, False])
        return self.local[-1]

    def wait(self, moves):
        for entry in moves:
            if not entry[1]:
                entry[0].wait()
                entry[1] = True

    def finish(self):
        for copy in self.remote:
            copy.wait_send()
        self.wait(self.local)


def normalized(values, gain, shift):
    center = values - jnp.mean(values, axis=-1, keepdims=True)
    spread = jnp.mean(center * center, axis=-1, keepdims=True)
    return center * lax.rsqrt(spread + EPSILON) * gain + shift


def head_masks(rows):
    lane = lax.broadcasted_iota(jnp.int32, (rows, PAIR), 1)
    first = (lane < HEAD_DIM).astype(F32).astype(BF)
    return first, (lane >= HEAD_DIM).astype(F32).astype(BF)


def both_heads(values, masks):
    return jnp.concatenate([values * masks[0], values * masks[1]], axis=0)


N_REMOTE1, N_LOCAL1 = 128, 80


def forward_kernel(
    shards,
    x_in, small_in, wq_in, wo_in, wu_in, wd_in,
    wq_all, wo_all, wu_all, wd_all,
    normed_out, q_out, kv_out, lse_out, att_out, res_out, nm_out, act_out, slope_out, small_out,
    xv, smv, normed, qv, kvb, lsev, att, res, nm, act, slope, wq, wo, wu,
    send_sems, recv_sems, local_sems,
):
    place = Place(shards)
    net = Copies(send_sems, recv_sems, local_sems)
    x, y, z, c = place.x, place.y, place.z, place.c
    slots, length, width = x_in.shape
    tokens = slots * length
    hidden = wu_in.shape[1]
    shard_rows = wq_in.shape[0]
    place.greet()

    small_moves = [net.move(small_in, smv.at[z])]
    small_sends = [net.send(small_in, smv.at[z], place.to_z(s)) for s in range(1, shards)]
    x_moves = [net.move(x_in, xv.at[0])]
    x_send = net.send(x_in, xv.at[1], place.to_y)

    def piece_rows(chunk, px, py, pc, lo=0, n=None):
        _, _, _, _, piece, rows, at = chunk
        n = rows if n is None else n
        return pl.ds(pl.multiple_of(((px * 2 + py) * 2 + pc) * piece + at + lo, 16), n)

    half = hidden // 2
    p32, pdn = shard_rows // 8, wd_in.shape[0] // 8
    chunks = [
        (wq_in, wq_all, width, width, p32, p32, 0),
        (wq_in, wq_all, 2 * width, width, p32, p32, 0),
        (wq_in, wq_all, 0, width, p32, p32, 0),
        (wo_in, wo_all, 0, width, p32, p32, 0),
        (wu_in, wu_all, 0, half, p32, p32, 0),
        (wu_in, wu_all, half, half, p32, p32, 0),
        (wd_in, wd_all, 0, width, pdn, pdn // 2, 0),
        (wd_in, wd_all, 0, width, pdn, pdn // 2, pdn // 2),
    ]
    state = [dict() for _ in chunks]
    others = pl.ds(1, shards - 1)

    def start_z(i):
        src, all_, col, cols, *_ = ch = chunks[i]
        rows = piece_rows(ch, x, y, c)
        cs = pl.ds(col, cols)
        state[i]["z"] = [
            net.send(src.at[rows, cs], all_.at[s, rows, cs], place.to_z(s)) for s in range(1, shards)
        ]

    def pass_piece(i, px, py, pc, lo, n, peer):
        _, all_, col, cols, *_ = ch = chunks[i]
        ref = all_.at[others, piece_rows(ch, px, py, pc, lo, n), pl.ds(col, cols)]
        return net.send(ref, ref, peer)

    def plane_one(i):
        rows = chunks[i][5]
        st = state[i]
        for copy in st["z"]:
            copy.wait_recv()
        st["x"] = pass_piece(i, x, y, c, 0, rows, place.to_x)
        st["y"] = pass_piece(i, x, y, c, 0, rows, place.to_y)
        st["core"] = [pass_piece(i, x, y, c, 0, rows, place.to_c)]

    def plane_two(i):
        rows = chunks[i][5]
        st = state[i]
        st["x"].wait_recv()
        st["xy"] = pass_piece(i, 1 - x, y, c, 0, rows // 2, place.to_y)
        st["core"].append(pass_piece(i, 1 - x, y, c, 0, rows, place.to_c))
        st["y"].wait_recv()
        st["yx"] = pass_piece(i, x, 1 - y, c, rows // 2, rows // 2, place.to_x)
        st["core"].append(pass_piece(i, x, 1 - y, c, 0, rows, place.to_c))

    def plane_three(i):
        rows = chunks[i][5]
        st = state[i]
        st["xy"].wait_recv()
        st["core"].append(pass_piece(i, 1 - x, 1 - y, c, 0, rows // 2, place.to_c))
        st["yx"].wait_recv()
        st["core"].append(pass_piece(i, 1 - x, 1 - y, c, rows // 2, rows // 2, place.to_c))

    def arrived(i):
        for copy in state[i]["core"]:
            copy.wait_recv()

    def load(i, dst):
        src, all_, col, cols, *_ = chunks[i]
        moves = []
        for s in range(shards):
            rows = pl.ds(pl.multiple_of(place.behind(s) * shard_rows, shard_rows), shard_rows)
            cs = pl.ds(col, cols)
            from_ = src.at[:, cs] if s == 0 else all_.at[s, :, cs]
            moves.append(net.move(from_, dst.at[rows, cs]))
        return moves

    start_z(0)
    start_z(1)

    net.wait(small_moves)
    for copy in small_sends:
        copy.wait_recv()
    small_moves = [net.move(smv, small_out)]

    def small(row, count=1):
        return jnp.concatenate([smv[s] for s in range(shards)], axis=1)[row : row + count].astype(F32)

    def norm_first(which):
        gain, shift = small(0), small(1)
        for slot in range(slots):
            rows = pl.ds(slot * length, length)
            normed[which, rows, :] = normalized(xv[which, slot].astype(F32), gain, shift).astype(BF)

    net.wait(x_moves)
    norm_first(0)
    plane_one(0)
    start_z(2)
    plane_one(1)
    plane_two(0)
    start_z(3)
    x_send.wait_recv()
    norm_first(1)
    moves_out = [net.move(normed, normed_out)]
    plane_one(2)
    plane_two(1)
    plane_three(0)
    start_z(4)
    arrived(0)
    k_moves = load(0, wq)
    plane_one(3)
    plane_two(2)
    plane_three(1)
    start_z(5)
    arrived(1)
    v_moves = load(1, wq)
    net.wait(k_moves)

    v_bias = small(3)

    def project_kv(which, part):
        lanes = pl.ds((part + 1) * width, width)
        rows = normed[which]
        out = dot(rows, wq[:, lanes])
        if part:
            out = out + v_bias
        out = out.astype(BF)
        at = (y if which == 0 else 1 - y) * 2 + c
        for slot in range(slots):
            kvb[slot, at, :, pl.ds(part * width, width)] = out[slot * length : (slot + 1) * length]

    shares = []

    def share(part):
        for which in range(2):
            at = (y if which == 0 else 1 - y) * 2 + c
            ref = kvb.at[:, at, :, pl.ds(part * width, width)]
            shares.append(net.send(ref, ref, place.to_c))

    project_kv(0, 0)
    project_kv(1, 0)
    share(0)
    plane_one(4)
    plane_two(3)
    plane_three(2)
    start_z(6)
    arrived(2)
    q_moves = load(2, wq)
    net.wait(v_moves)
    project_kv(0, 1)
    project_kv(1, 1)
    share(1)
    plane_three(3)
    arrived(3)
    o_moves = load(3, wo)
    net.wait(q_moves)
    qv[...] = (dot(normed[0], wq[:, :width]) + small(2)).astype(BF)
    moves_out.append(net.move(qv, q_out))
    plane_one(5)
    plane_two(4)
    start_z(7)
    for copy in shares:
        copy.wait_recv()
    moves_out.append(net.move(kvb, kv_out))

    def attend(slot, lo, hi):
        masks = head_masks(length)

        @pl.loop(lo, hi)
        def _(p):
            lanes = pl.ds(pl.multiple_of(p * PAIR, PAIR), PAIR)
            v_lanes = pl.ds(pl.multiple_of(width + p * PAIR, PAIR), PAIR)
            rows = pl.ds(slot * length, length)
            queries = both_heads(qv[rows, lanes] * BF(HEAD_DIM**-0.5), masks)
            keys = kvb[slot, :, :, lanes].reshape(-1, PAIR)
            values = kvb[slot, :, :, v_lanes].reshape(-1, PAIR)
            scores = dot(keys, queries, NT)
            top = jnp.max(scores, axis=0, keepdims=True)
            terms = jnp.exp(scores - top)
            total = jnp.sum(terms, axis=0, keepdims=True)
            lsev[slot, p] = top + jnp.log(total)
            out = dot(values, terms.astype(BF), TN) * (1.0 / total)
            out = jnp.concatenate([out[:HEAD_DIM, :length], out[HEAD_DIM:, length:]], axis=0)
            att[rows, lanes] = out.T.astype(BF)

    pairs = width // PAIR
    attend(0, 0, pairs)
    plane_one(6)
    plane_two(5)
    plane_three(4)
    arrived(4)
    up_moves = [load(4, wu)]
    attend(1, 0, pairs)
    moves_out += [net.move(lsev, lse_out), net.move(att, att_out)]
    plane_one(7)
    plane_two(6)
    plane_three(5)
    arrived(5)
    up_moves.append(load(5, wu))

    net.wait(o_moves)
    out_bias, mlp_gain, mlp_shift = small(4), small(5), small(6)
    for slot in range(slots):
        rows = pl.ds(slot * length, length)
        value = xv[0, slot].astype(F32) + dot(att[rows], wo[...]) + out_bias
        res[rows] = value
        nm[rows] = normalized(value, mlp_gain, mlp_shift).astype(BF)
    moves_out += [net.move(res, res_out), net.move(nm, nm_out)]

    up_block = 512

    def up(part):
        @pl.loop(part * (half // up_block), (part + 1) * (half // up_block))
        def _(j):
            lanes = pl.ds(pl.multiple_of(j * up_block, up_block), up_block)
            s, inner = j // (wd_in.shape[0] // up_block), j % (wd_in.shape[0] // up_block)
            first = 8 + inner * (up_block // shard_rows)
            sm = smv[s].astype(F32)
            row = jnp.concatenate([sm[8:9], sm[9:10]], axis=1)
            row2 = jnp.concatenate([sm[10:11], sm[11:12]], axis=1)
            bias = jnp.where(inner == 0, row, row2)
            pre = dot(nm[...], wu[:, lanes]) + bias
            phi = 0.5 + 0.5 * lax.erf(pre * (0.5**0.5))
            density = jnp.exp(pre * pre * -0.5) * 0.3989422804014327
            act[:, lanes] = (pre * phi).astype(BF)
            slope[:, lanes] = (phi + pre * density).astype(BF)

    net.wait(up_moves[0])
    up(0)
    plane_two(7)
    plane_three(6)
    net.wait(up_moves[1])
    up(1)
    moves_out += [net.move(act, act_out), net.move(slope, slope_out)]
    plane_three(7)
    arrived(6)
    arrived(7)
    net.finish()


def forward(shards, x, small, wq, wo, wu, wd):
    slots, length, width = x.shape
    tokens = slots * length
    rows = wq.shape[0]
    hidden = wu.shape[1]
    pairs = width // PAIR
    clip = 4 * length
    any_ = pl.BlockSpec(memory_space=pl.ANY)
    sd = jax.ShapeDtypeStruct
    outs = (
        sd((shards,) + wq.shape, BF), sd((shards,) + wo.shape, BF), sd((shards,) + wu.shape, BF), sd((shards,) + wd.shape, BF),
        sd((2, tokens, width), BF), sd((tokens, width), BF), sd((slots, 4, length, 2 * width), BF),
        sd((slots, pairs, 1, 2 * length), F32), sd((tokens, width), BF), sd((tokens, width), F32),
        sd((tokens, width), BF), sd((tokens, hidden), BF), sd((tokens, hidden), BF), sd((shards,) + small.shape, BF),
    )
    return pl.pallas_call(
        functools.partial(forward_kernel, shards),
        out_shape=outs,
        in_specs=[any_] * 6,
        out_specs=(any_,) * len(outs),
        scratch_shapes=[
            pltpu.VMEM((2, slots, length, width), BF),
            pltpu.VMEM((shards,) + small.shape, BF),
            pltpu.VMEM((2, tokens, width), BF),
            pltpu.VMEM((tokens, width), BF),
            pltpu.VMEM((slots, 4, length, 2 * width), BF),
            pltpu.VMEM((slots, pairs, 1, 2 * length), F32),
            pltpu.VMEM((tokens, width), BF),
            pltpu.VMEM((tokens, width), F32),
            pltpu.VMEM((tokens, width), BF),
            pltpu.VMEM((tokens, hidden), BF),
            pltpu.VMEM((tokens, hidden), BF),
            pltpu.VMEM((width, 3 * width), BF),
            pltpu.VMEM((width, width), BF),
            pltpu.VMEM((width, hidden), BF),
            pltpu.SemaphoreType.DMA((N_REMOTE1,)),
            pltpu.SemaphoreType.DMA((N_REMOTE1,)),
            pltpu.SemaphoreType.DMA((N_LOCAL1,)),
        ],
        compiler_params=pltpu.CompilerParams(collective_id=1, has_side_effects=True, vmem_limit_bytes=62 * MIB),
    )(x, small, wq, wo, wu, wd)


def contract_rows(left, right):
    return lax.dot_general(left, right, TN, preferred_element_type=F32)


def contract_cols(left, right):
    return lax.dot_general(left, right, NT, preferred_element_type=F32)


def row_total(values):
    return jnp.sum(values.astype(F32), axis=0)


def norm_pull(values, gain, shift, incoming):
    _, pull = jax.vjp(normalized, values, gain, shift)
    return pull(incoming)


def local(
    activations, cotangent, clip_loads, attn_gain, attn_shift, w_qkv, q_bias, v_bias, w_out, out_bias,
    mlp_gain, mlp_shift, w_up, up_bias, w_down, down_bias,
):
    shards = lax.axis_size("shard")
    z = lax.axis_index("shard")
    x = activations[0]
    slots, length, width = x.shape
    tokens = slots * length
    heads = width // HEAD_DIM
    rows = w_qkv.shape[0]
    vectors = [attn_gain, attn_shift, q_bias, v_bias, out_bias, mlp_gain, mlp_shift, down_bias]
    small = jnp.concatenate([jnp.stack(vectors), up_bias.reshape(-1, rows)], axis=0)
    small = jnp.pad(small, ((0, 16 - small.shape[0]), (0, 0)))
    (wq, wo, wu, wd, normed, q, kv, lse, att, res, nm, act, slope, smalls) = forward(
        shards, x, small, w_qkv, w_out, w_up, w_down
    )
    order = (z - jnp.arange(shards)) % shards

    def whole(gathered, own):
        return gathered.at[0].set(own)[order].reshape((-1,) + own.shape[1:])

    wq, wo, wu, wd = whole(wq, w_qkv), whole(wo, w_out), whole(wu, w_up), whole(wd, w_down)
    full = jnp.concatenate([smalls[s] for s in range(shards)], axis=1).astype(F32)
    live = (jnp.arange(slots) < clip_loads[0]).astype(F32)[:, None, None]
    live = jnp.broadcast_to(live, (slots, length, 1)).reshape(tokens, 1)
    out_grad = cotangent[0].reshape(tokens, width).astype(F32) * live
    layer_out = (live * (res + jnp.dot(act, wd, preferred_element_type=F32) + full[7:8])).astype(BF)
    d_mlp = out_grad.astype(BF)
    grad_w_down = contract_rows(act, d_mlp)
    grad_down_bias = row_total(d_mlp)
    d_pre = (contract_cols(d_mlp, wd) * slope.astype(F32)).astype(BF)
    grad_w_up = contract_rows(nm, d_pre)
    grad_up_bias = row_total(d_pre)
    d_norm = contract_cols(d_pre, wu)
    d_res_norm, grad_mlp_gain, grad_mlp_shift = norm_pull(res, full[5], full[6], d_norm)
    d_residual = out_grad + d_res_norm
    d_branch = d_residual.astype(BF)
    grad_w_out = contract_rows(att, d_branch)
    grad_out_bias = row_total(d_branch)
    d_att = contract_cols(d_branch, wo).astype(BF)
    scale = HEAD_DIM**-0.5
    d_q, d_kv = [], []
    for slot in range(slots):
        span = slice(slot * length, (slot + 1) * length)
        queries = q[span].reshape(length, heads, HEAD_DIM)
        keys = kv[slot, :, :, :width].reshape(-1, heads, HEAD_DIM)
        values = kv[slot, :, :, width:].reshape(-1, heads, HEAD_DIM)
        d_a = d_att[span].reshape(length, heads, HEAD_DIM)
        logs = lse[slot].reshape(heads, length)
        scores = jnp.einsum("thd,lhd->htl", queries, keys, preferred_element_type=F32) * scale
        probs = jnp.exp(scores - logs[:, :, None])
        d_probs = jnp.einsum("thd,lhd->htl", d_a, values, preferred_element_type=F32)
        d_scores = (probs * (d_probs - jnp.sum(probs * d_probs, axis=-1, keepdims=True))).astype(BF)
        d_q.append(jnp.einsum("htl,lhd->thd", d_scores, keys, preferred_element_type=F32).reshape(length, width) * scale)
        d_k = jnp.einsum("htl,thd->lhd", d_scores, queries, preferred_element_type=F32) * scale
        d_v = jnp.einsum("htl,thd->lhd", probs.astype(BF), d_a, preferred_element_type=F32)
        d_kv.append(jnp.concatenate([d_k.reshape(-1, width), d_v.reshape(-1, width)], axis=1).astype(BF))
    d_q = jnp.concatenate(d_q).astype(BF)
    d_kv = jnp.stack(d_kv).reshape(slots, 4, length, 2 * width)
    d_kv = lax.psum_scatter(d_kv, "seq", scatter_dimension=1, tiled=True).reshape(tokens, 2 * width)
    d_project = jnp.concatenate([d_q, d_kv], axis=1)
    grad_w_qkv = contract_rows(normed[0], d_project)
    grad_q_bias = row_total(d_q)
    grad_v_bias = row_total(d_kv[:, width:])
    d_norm1 = contract_cols(d_project, wq)
    d_in, grad_attn_gain, grad_attn_shift = norm_pull(x.reshape(tokens, width).astype(F32), full[0], full[1], d_norm1)
    input_grad = (d_residual + d_in).astype(BF)

    def scatter(value):
        value = lax.psum_scatter(value.astype(BF), ("shard", "seq"), scatter_dimension=0, tiled=True)
        return lax.psum(value, "replica").astype(F32)

    def total(value):
        value = lax.psum(value, ("replica", "shard", "seq"))
        n = value.shape[0] // (shards * lax.axis_size("seq"))
        at = z * lax.axis_size("seq") + lax.axis_index("seq")
        return lax.dynamic_slice_in_dim(value, at * n, n)

    shape = activations.shape
    return (
        layer_out.reshape(shape), input_grad.reshape(shape), total(grad_attn_gain), total(grad_attn_shift),
        scatter(grad_w_qkv), total(grad_q_bias), total(grad_v_bias), scatter(grad_w_out), total(grad_out_bias),
        total(grad_mlp_gain), total(grad_mlp_shift), scatter(grad_w_up), total(grad_up_bias),
        scatter(grad_w_down), total(grad_down_bias),
    )


def solution(mesh):
    rows = P("shard")
    full = P("shard", None)
    clips = P(("replica", "shard"), None, "seq", None)
    vec = P(("shard", "seq"))
    mat = P(("shard", "seq"), None)
    return jax.shard_map(
        local,
        mesh=mesh,
        in_specs=(
            clips, clips, P(("replica", "shard")), rows, rows, full, rows, rows, full, rows, rows, rows, full, rows, full, rows,
        ),
        out_specs=(clips, clips, vec, vec, mat, vec, vec, mat, vec, vec, vec, mat, vec, mat, vec),
        check_vma=False,
    )
```

time: 1420 us -> 896 us (0.63)
  waiting for transfers between devices: 885 us -> 371 us
  matrix products: 244 us -> 123 us
  Pallas kernels: 0 us -> 121 us
  blocking collectives: 154 us -> 41.6 us
  local copies, waits for them, and re-layouts: 47.3 us -> 158 us
    all_gather x8 -> x0, waiting for transfers between devices: 374 us -> none  [the longest x1 130 us: local(): lax.all_gather(w_up, 'shard', axis=0, tiled=True)]
    reduce_scatter x6 -> x5, waiting for transfers between devices: 506 us -> 371 us  [the longest x4 331 us: scatter(): lax.psum_scatter(value.astype(BF), ('shard', 'seq'), scatter_dimension=0,...]
    pallas_call x0 -> x1, Pallas kernels: none -> 121 us  [forward(): pl.pallas_call(functools.partial(forward_kernel, shards), out_shape=outs,...]
    dot_general x36 -> x19, matrix products: 244 us -> 123 us  [the longest x4 28.4 us: contract_rows(): return lax.dot_general(left, right, TN, preferred_element_type=F32)]
    all_gather x9 -> x0, blocking collectives: 88.9 us -> none  [the longest x1 14.4 us: local(): lax.all_gather(attn_shift, 'shard', axis=0, tiled=True)]
    unnamed x1 -> x0, blocking collectives: 59.8 us -> none
    gather x0 -> x8, local copies, waits for them, and re-layouts: none -> 42.4 us  [whole(): return gathered.at[0].set(own)[order].reshape((-1,) + own.shape[1:])]
    psum x1, blocking collectives: 4.98 us -> 41.6 us  [total(): value = lax.psum(value, ('replica', 'shard', 'seq'))]
  transfers between devices with their start and end apart: 15 -> 6, of which waited for: 9 -> 5; matrix products, arithmetic and copies ran while one was open for 17% -> 10% of each run, Pallas kernels for 0% -> 0%
where the time goes in v1:
time: 896 us; the launch traced here: 889 us
  waiting for transfers between devices  371 us (41%)
  local copies, waits for them, and re-layouts  158 us (18%)
  matrix products  123 us (14%)
  Pallas kernels  121 us (14%)
  other arithmetic  57.4 us (6%)
  blocking collectives  41.6 us (5%)
  between operations  15.7 us (2%)
    reduce_scatter x4, waiting for transfers between devices, scatter(): lax.psum_scatter(value.astype(BF), ('shard', 'seq'), scatter_dimension=0,...  331 us
    pallas_call x1, Pallas kernels, forward(): pl.pallas_call(functools.partial(forward_kernel, shards), out_shape=outs,...  121 us
    gather x8, local copies, waits for them, and re-layouts, whole(): return gathered.at[0].set(own)[order].reshape((-1,) + own.shape[1:])  42.4 us
    psum x1, blocking collectives, total(): value = lax.psum(value, ('replica', 'shard', 'seq'))  41.6 us
    reduce_scatter x1, waiting for transfers between devices, local(): lax.psum_scatter(d_kv, 'seq', scatter_dimension=1, tiled=True)  40.1 us
    concatenate x8, local copies, waits for them, and re-layouts, local(): jnp.concatenate([d_k.reshape(-1, width), d_v.reshape(-1, width)], axis=1)  29 us
    dot_general x4, matrix products, contract_rows(): return lax.dot_general(left, right, TN, preferred_element_type=F32)  28.4 us
    dot_general x4, matrix products, contract_cols(): return lax.dot_general(left, right, NT, preferred_element_type=F32)  27.8 us
  transfers between devices with their start and end apart: 6, of which 5 were waited for; matrix products, arithmetic and copies ran while one was open for 10% of the time, Pallas kernels for 0%

profile of v1, /device:TPU:0, one launch (start us, length us, event | category | flops | bytes accessed | tf_op | source)
XLA Modules:
  0.0 888.9 jit_solution(3822408073168715396)
XLA Ops:
  17.8 120.6 %shard_map.271 = (bf16[4,256,3072]{2,1,0:T(8,128)(2,1)}, bf16[4,256,1024]{2,1,0:T(8,128)(2,1)}, bf16[4,256,4096]{2,1,0:T(8,128)(2,1)}, bf16[4,1024,1024]{2,1,0:T...) custom-call(bf16[2,256,1024]{2,1,0:T(8,128)(2,1)} %bitcast.134, ...), custom_call_target="tpu_custom_call" | custom-call | tf_op jit(solution)/shard_map/pallas_call | solution.py:378
  188.3 7.7 pad_maximum_fusion
  196.0 7.9 pad_maximum_fusion.1
  203.9 11.1 %convert_reduce_fusion = (f32[4096]{0:T(1024)}, bf16[512,4096]{1,0:T(8,128)(2,1)}) fusion(bf16[512,4096]{1,0:T(8,128)(2,1)} %get-tuple-element.81, bf16[512,1024]{1,0:T(8,128)(2,1)S(1)} %bitcast.150, bf16[4096,1024]{1,0:T(8,128)(2,1)} %bitcast.135), kind=kOutput, calls=%fused_computation.19 | convolution fusion | flops 4305448960 | bytes 17842176 | tf_op jit(solution)/shard_map/dot_general | solution.py:411
  215.6 7.6 multiply_reduce_fusion.2
  281.1 10.3 %multiply_reduce_fusion.1 = (f32[16,256]{1,0:T(8,128)}, f32[16,256,1024]{2,1,0:T(8,128)S(1)}) fusion(f32[16,256,1024]{2,1,0:T(8,128)} %copy-done, f32[16,256]{1,0:T(8,128)} %sub.74, bf16[256,16,64]{0,2,1:T(8,128)(2,1)} %bitcast.145, bf16[1024,16,64]{0,2,1:T(8,128)(2,1)} %reshape_squeeze.15), kind=kOutput, calls=%fused_computation.10 | convolution fusion | flops 553644032 | bytes 36208640 | tf_op jit(solution)/shard_map/thd,lhd->htl/dot_general | solution.py:475
  291.4 8.0 multiply_convert_fusion.1
  334.5 10.3 %multiply_reduce_fusion = (f32[16,256]{1,0:T(8,128)}, f32[16,256,1024]{2,1,0:T(8,128)S(1)}) fusion(f32[16,256,1024]{2,1,0:T(8,128)} %copy-done.1, f32[16,256]{1,0:T(8,128)} %sub.79, bf16[256,16,64]{0,2,1:T(8,128)(2,1)} %bitcast.143, bf16[1024,16,64]{0,2,1:T(8,128)(2,1)} %reshape_squeeze.17), kind=kOutput, calls=%fused_computation.7 | convolution fusion | flops 553644032 | bytes 36208640 | tf_op jit(solution)/shard_map/thd,lhd->htl/dot_general | solution.py:475
  344.8 8.0 multiply_convert_fusion
  364.8 6.5 maximum_maximum_fusion
  376.6 9.5 %convolution_convert_fusion.1 = bf16[1024,4096]{1,0:T(8,128)(2,1)} fusion(bf16[512,1024]{1,0:T(8,128)(2,1)S(1)} %copy-done.45, bf16[512,4096]{1,0:T(8,128)(2,1)} %get-tuple-element.151), kind=kOutput, calls=%fused_computation.26 | convolution fusion | flops 4299161600 | bytes 13631488 | tf_op jit(solution)/shard_map/dot_general | solution.py:407
  386.4 8.7 fusion.17
  397.1 7.1 fusion.18
  405.5 40.1 %reduce-scatter.6.cloned.1.call-done = bf16[2,1,256,2048]{3,2,0,1:T(8,128)(2,1)} async-done(((bf16[2,4,256,2048]{3,2,0,1:T(8,128)(2,1)}), bf16[2,1,256,2048]{3,2,0,1:T(8,128)(2,1)}) %reduce-scatter.6.cloned.1.call-update) | async-done | bytes 2097168 | tf_op jit(solution)/shard_map/reduce_scatter | solution.py:483
  445.5 8.2 convolution_convert_fusion.2
  458.3 6.8 gather_fusion.1
  465.1 7.9 fusion.33
  477.1 6.7 convolution_convert_fusion
  485.2 26.1 %reduce-scatter.10.cloned.1.call-done = bf16[64,1024]{1,0:T(8,128)(2,1)} async-done(((bf16[1024,1024]{1,0:T(8,128)(2,1)}), bf16[64,1024]{1,0:T(8,128)(2,1)}) %reduce-scatter.10.cloned.1.call-update) | async-done | bytes 131088 | tf_op jit(solution)/shard_map/reduce_scatter | solution.py:493
  511.3 107.7 %reduce-scatter.12.cloned.1.call-done = bf16[64,4096]{1,0:T(8,128)(2,1)} async-done(((bf16[1024,4096]{1,0:T(8,128)(2,1)}), bf16[64,4096]{1,0:T(8,128)(2,1)}) %reduce-scatter.12.cloned.1.call-update) | async-done | bytes 524304 | tf_op jit(solution)/shard_map/reduce_scatter | solution.py:493
  619.1 88.8 %reduce-scatter.8.cloned.1.call-done = bf16[64,3072]{1,0:T(8,128)(2,1)} async-done(((bf16[1024,3072]{1,0:T(8,128)(2,1)}), bf16[64,3072]{1,0:T(8,128)(2,1)}) %reduce-scatter.8.cloned.1.call-update) | async-done | bytes 393232 | tf_op jit(solution)/shard_map/reduce_scatter | solution.py:493
  707.9 108.4 %reduce-scatter.14.cloned.1.call-done = bf16[256,1024]{1,0:T(8,128)(2,1)} async-done(((bf16[4096,1024]{1,0:T(8,128)(2,1)}), bf16[256,1024]{1,0:T(8,128)(2,1)}) %reduce-scatter.14.cloned.1.call-update) | async-done | bytes 524304 | tf_op jit(solution)/shard_map/reduce_scatter | solution.py:493
  816.4 10.2 %multiply_convert_fusion.6 = bf16[512,1024]{1,0:T(8,128)(2,1)} fusion(f32[512,1024]{1,0:T(8,128)S(1)} %copy-done.6, bf16[512,4096]{1,0:T(8,128)(2,1)} %get-tuple-element.78, bf16[4096,1024]{1,0:T(8,128)(2,1)} %bitcast.136, f32[1024]{0:T(1024)S(1)} %bitcast.167, f32[512]{0:T(512)S(1)} %bitcast.160), kind=kOutput, calls=%fused_computation.52 | convolution fusion | flops 4297064448 | bytes 15734784 | tf_op jit(solution)/shard_map/dot_general | solution.py:450
  826.9 41.6 %all-reduce.1 = (f32[1024]{0:T(1024)S(1)}, f32[1024]{0:T(1024)S(1)}, f32[1024]{0:T(1024)S(1)}, f32[1024]{0:T(1024)S(1)}, f32[1024]{0:T(1024)S(1)}, /*index=5*/f3...) all-reduce(f32[1024]{0:T(1024)S(1)} %copy-done.35, ...), channel_id=1, replica_groups=mesh['replica'=2,'shard'=4,'seq'=4] {'replica','shard','seq'}, use_global_device_ids=true, to_apply=%region_12.13 | all-reduce | flops 12288 | bytes 98304 | tf_op jit(solution)/shard_map/psum | solution.py:497
  (204 shorter events, 197.5 us)
Async XLA Ops:
  7.2 438.3 %reduce-scatter.6.cloned.1.call-start = ((), (), s32[]{:S(2)}) async-start(), calls=%async_computation.5 | async-start | bytes 10485760 | tf_op jit(solution)/shard_map/reduce_scatter | solution.py:483
  13.9 169.4 %copy-start.38 = (s32[1024]{0:T(1024)}, s32[1024]{0:T(1024)S(1)}, u32[]{:S(2)}) copy-start(s32[1024]{0:T(1024)S(1)} %pad_clamp_fusion) | copy-start | bytes 12292
  148.2 67.3 %copy-start.39 = (f32[512]{0:T(512)}, f32[512]{0:T(512)S(1)}, u32[]{:S(2)}) copy-start(f32[512]{0:T(512)S(1)} %fusion.24) | copy-start | bytes 6148
  203.9 11.7 %copy-start.13 = (bf16[4,256,4096]{2,1,0:T(8,128)(2,1)S(1)}, bf16[4,256,4096]{2,1,0:T(8,128)(2,1)}, u32[]{:S(2)}) copy-start(bf16[4,256,4096]{2,1,0:T(8,128)(2,1)} %pad_maximum_fusion.1) | copy-start | bytes 25165828
  260.7 9.7 %copy-start.18 = (bf16[256,1024]{0,1:T(8,128)(2,1)S(1)}, bf16[256,1024]{0,1:T(8,128)(2,1)}, u32[]{:S(2)}) copy-start(bf16[256,1024]{0,1:T(8,128)(2,1)} %copy.48) | copy-start | bytes 1572868
  291.4 11.2 %copy-start.16 = (bf16[256,1024]{0,1:T(8,128)(2,1)S(1)}, bf16[256,1024]{0,1:T(8,128)(2,1)}, u32[]{:S(2)}) copy-start(bf16[256,1024]{0,1:T(8,128)(2,1)} %copy.47) | copy-start | bytes 1572868
  344.8 11.3 %copy-start.15 = (bf16[256,1024]{0,1:T(8,128)(2,1)S(1)}, bf16[256,1024]{0,1:T(8,128)(2,1)}, u32[]{:S(2)}) copy-start(bf16[256,1024]{0,1:T(8,128)(2,1)} %copy.51) | copy-start | bytes 1572868
  371.3 140.0 %reduce-scatter.10.cloned.1.call-start = ((), (), s32[]{:S(2)}) async-start(), calls=%async_computation.7 | async-start | bytes 2228224 | tf_op jit(solution)/shard_map/reduce_scatter | solution.py:493
  376.5 242.5 %reduce-scatter.12.cloned.1.call-start = ((), (), s32[]{:S(2)}) async-start(), calls=%async_computation.8 | async-start | bytes 8912896 | tf_op jit(solution)/shard_map/reduce_scatter | solution.py:493
  386.1 11.0 %copy-start.8 = (bf16[1024,16,64]{0,2,1:T(8,128)(2,1)S(1)}, bf16[1024,16,64]{0,2,1:T(8,128)(2,1)}, u32[]{:S(2)}) copy-start(bf16[1024,16,64]{0,2,1:T(8,128)(2,1)} %reshape_squeeze.16) | copy-start | bytes 6291460
  386.2 321.7 %reduce-scatter.8.cloned.1.call-start = ((), (), s32[]{:S(2)}) async-start(), calls=%async_computation.6 | async-start | bytes 6684672 | tf_op jit(solution)/shard_map/reduce_scatter | solution.py:493
  405.4 59.6 %copy-start.23 = (bf16[256,1024]{1,0:T(8,128)(2,1)}, bf16[256,1024]{1,0:T(8,128)(2,1)S(1)}, u32[]{:S(2)}) copy-start(bf16[256,1024]{1,0:T(8,128)(2,1)S(1)} %copy.55) | copy-start | bytes 1572868
  453.7 362.5 %reduce-scatter.14.cloned.1.call-start = ((), (), s32[]{:S(2)}) async-start(), calls=%async_computation.9 | async-start | bytes 8912896 | tf_op jit(solution)/shard_map/reduce_scatter | solution.py:493
  483.8 332.4 %copy-start.6 = (f32[512,1024]{1,0:T(8,128)S(1)}, f32[512,1024]{1,0:T(8,128)}, u32[]{:S(2)}) copy-start(f32[512,1024]{1,0:T(8,128)} %get-tuple-element.77) | copy-start | bytes 6291460
  483.8 332.4 %copy-start.43 = (f32[1,1024]{1,0:T(1,128)S(1)}, f32[1,1024]{1,0:T(1,128)}, u32[]{:S(2)}) copy-start(f32[1,1024]{1,0:T(1,128)} %get-tuple-element.135) | copy-start | bytes 12292
  483.9 389.9 %all-reduce.5.cloned.1.call-start = ((), (), s32[]{:S(2)}) async-start(), calls=%async_computation.10 | async-start | bytes 3145728 | tf_op jit(solution)/shard_map/psum | solution.py:494
  816.3 10.3 %copy-start.28 = (bf16[2,1,256,2048]{3,2,0,1:T(8,128)(2,1)S(1)}, bf16[2,1,256,2048]{3,2,0,1:T(8,128)(2,1)}, u32[]{:S(2)}) copy-start(bf16[2,1,256,2048]{3,2,0,1:T(8,128)(2,1)} %reduce-scatter.6.cloned.1.call-done) | copy-start | bytes 6291460
  816.3 10.5 %copy-start.34 = (f32[1024]{0:T(1024)S(1)}, f32[1024]{0:T(1024)}, u32[]{:S(2)}) copy-start(f32[1024]{0:T(1024)} %get-tuple-element.113) | copy-start | bytes 12292
  816.3 10.5 %copy-start.35 = (f32[1024]{0:T(1024)S(1)}, f32[1024]{0:T(1024)}, u32[]{:S(2)}) copy-start(f32[1024]{0:T(1024)} %get-tuple-element.93) | copy-start | bytes 12292
  816.3 10.5 %copy-start.36 = (f32[4096]{0:T(1024)S(1)}, f32[4096]{0:T(1024)}, u32[]{:S(2)}) copy-start(f32[4096]{0:T(1024)} %get-tuple-element.150) | copy-start | bytes 49156
  816.3 10.5 %copy-start.37 = (f32[1024]{0:T(1024)S(1)}, f32[1024]{0:T(1024)}, u32[]{:S(2)}) copy-start(f32[1024]{0:T(1024)} %get-tuple-element.115) | copy-start | bytes 12292
  816.3 10.5 %copy-start.40 = (f32[1024]{0:T(1024)S(1)}, f32[1024]{0:T(1024)}, u32[]{:S(2)}) copy-start(f32[1024]{0:T(1024)} %get-tuple-element.91) | copy-start | bytes 12292
  816.4 10.5 %copy-start.41 = (f32[1024]{0:T(1024)S(1)}, f32[1024]{0:T(1024)}, u32[]{:S(2)}) copy-start(f32[1024]{0:T(1024)} %get-tuple-element.95) | copy-start | bytes 12292
  816.4 10.5 %copy-start.42 = (f32[1024]{0:T(1024)S(1)}, f32[1024]{0:T(1024)}, u32[]{:S(2)}) copy-start(f32[1024]{0:T(1024)} %get-tuple-element.96) | copy-start | bytes 12292
  (28 other events, 120.7 us)
Sparse Core Ops, SparseCore 0:
  371.5 74.0 reduce-scatter.5
  449.7 61.5 reduce-scatter.9
  515.4 103.5 reduce-scatter.11
  622.8 84.9 reduce-scatter.7
  712.3 103.8 reduce-scatter.13
  818.7 53.1 all-reduce.4

commit v2 on v1

--- a/solution.py
+++ b/solution.py
@@ -1,5 +1,4 @@
 import functools
-
 import jax
 import jax.numpy as jnp
 from jax import lax
@@ -249,14 +248,14 @@
         out = out.astype(BF)
         at = (y if which == 0 else 1 - y) * 2 + c
         for slot in range(slots):
-            kvb[slot, at, :, pl.ds(part * width, width)] = out[slot * length : (slot + 1) * length]
+            kvb[slot, part, at] = out[slot * length : (slot + 1) * length]
 
     shares = []
 
     def share(part):
         for which in range(2):
             at = (y if which == 0 else 1 - y) * 2 + c
-            ref = kvb.at[:, at, :, pl.ds(part * width, width)]
+            ref = kvb.at[:, part, at]
             shares.append(net.send(ref, ref, place.to_c))
 
     project_kv(0, 0)
@@ -291,11 +290,10 @@
         @pl.loop(lo, hi)
         def _(p):
             lanes = pl.ds(pl.multiple_of(p * PAIR, PAIR), PAIR)
-            v_lanes = pl.ds(pl.multiple_of(width + p * PAIR, PAIR), PAIR)
             rows = pl.ds(slot * length, length)
             queries = both_heads(qv[rows, lanes] * BF(HEAD_DIM**-0.5), masks)
-            keys = kvb[slot, :, :, lanes].reshape(-1, PAIR)
-            values = kvb[slot, :, :, v_lanes].reshape(-1, PAIR)
+            keys = kvb[slot, 0, :, :, lanes].reshape(-1, PAIR)
+            values = kvb[slot, 1, :, :, lanes].reshape(-1, PAIR)
             scores = dot(keys, queries, NT)
             top = jnp.max(scores, axis=0, keepdims=True)
             terms = jnp.exp(scores - top)
@@ -363,15 +361,13 @@
 def forward(shards, x, small, wq, wo, wu, wd):
     slots, length, width = x.shape
     tokens = slots * length
-    rows = wq.shape[0]
     hidden = wu.shape[1]
     pairs = width // PAIR
-    clip = 4 * length
     any_ = pl.BlockSpec(memory_space=pl.ANY)
     sd = jax.ShapeDtypeStruct
     outs = (
         sd((shards,) + wq.shape, BF), sd((shards,) + wo.shape, BF), sd((shards,) + wu.shape, BF), sd((shards,) + wd.shape, BF),
-        sd((2, tokens, width), BF), sd((tokens, width), BF), sd((slots, 4, length, 2 * width), BF),
+        sd((2, tokens, width), BF), sd((tokens, width), BF), sd((slots, 2, 4, length, width), BF),
         sd((slots, pairs, 1, 2 * length), F32), sd((tokens, width), BF), sd((tokens, width), F32),
         sd((tokens, width), BF), sd((tokens, hidden), BF), sd((tokens, hidden), BF), sd((shards,) + small.shape, BF),
     )
@@ -385,7 +381,7 @@
             pltpu.VMEM((shards,) + small.shape, BF),
             pltpu.VMEM((2, tokens, width), BF),
             pltpu.VMEM((tokens, width), BF),
-            pltpu.VMEM((slots, 4, length, 2 * width), BF),
+            pltpu.VMEM((slots, 2, 4, length, width), BF),
             pltpu.VMEM((slots, pairs, 1, 2 * length), F32),
             pltpu.VMEM((tokens, width), BF),
             pltpu.VMEM((tokens, width), F32),
@@ -403,108 +399,542 @@
     )(x, small, wq, wo, wu, wd)
 
 
-def contract_rows(left, right):
-    return lax.dot_general(left, right, TN, preferred_element_type=F32)
-
-
-def contract_cols(left, right):
-    return lax.dot_general(left, right, NT, preferred_element_type=F32)
-
-
-def row_total(values):
-    return jnp.sum(values.astype(F32), axis=0)
-
-
-def norm_pull(values, gain, shift, incoming):
-    _, pull = jax.vjp(normalized, values, gain, shift)
-    return pull(incoming)
+N_REMOTE2, N_LOCAL2 = 160, 80
+RING_A, RING_B = 3, 5
+
+
+def norm_back(values, gain, incoming):
+    center = values - jnp.mean(values, axis=-1, keepdims=True)
+    spread = jnp.mean(center * center, axis=-1, keepdims=True)
+    r = lax.rsqrt(spread + EPSILON)
+    xhat = center * r
+    e = incoming * gain
+    back = r * (e - jnp.mean(e, axis=-1, keepdims=True) - xhat * jnp.mean(e * xhat, axis=-1, keepdims=True))
+    return back, incoming * xhat
+
+
+def col_sum(values):
+    return jnp.sum(values.astype(F32), axis=0, keepdims=True)
+
+
+def backward_kernel(
+    shards,
+    x_in, cot_in, live_in, small_in, wq_in, wo_in, wu_in, wd_in, wq_all, wo_all, wu_all, wd_all,
+    normed_in, q_in, kv_in, lse_in, att_in, res_in, nm_in, act_in, slope_in,
+    layer_out, input_out, gq_out, go_out, gu_out, gd_out, sg_out,
+    wa, wb, ad, nm, att, res, dm, dbr, qv, normed, xv, dn, lsev,
+    gq, go, gu, gd, sg, ub, sr,
+    gbuf, r0, r1x, r1y, r2x, r2y, r3, r4, fbuf, tbuf,
+    send_sems, recv_sems, local_sems, free_sems, act_free,
+):
+    place = Place(shards)
+    net = Copies(send_sems, recv_sems, local_sems)
+    x, y, z, c = place.x, place.y, place.z, place.c
+    slots, length, width = x_in.shape
+    tokens = slots * length
+    hidden = wu_in.shape[1]
+    shard_rows = wq_in.shape[0]
+    down_rows = wd_in.shape[0]
+    block = 256
+    clip = 4 * length
+
+    def span(slot):
+        return pl.ds(slot * length, length)
+
+    cot_moves = [net.move(cot_in.at[slot], dm.at[span(slot)]) for slot in range(slots)]
+    act_moves = [net.move(act_in, ad.at[0])]
+
+    def blocks_of(own, gathered, cols, dst_of):
+        moves = []
+        for s in range(shards):
+            src = own.at[:, cols] if s == 0 else gathered.at[s, :, cols]
+            moves.append(net.move(src, dst_of(place.behind(s))))
+        return moves
+
+    every = pl.ds(0, width)
+    wd_moves = blocks_of(
+        wd_in, wd_all, every, lambda a: wa.at[pl.ds(pl.multiple_of(a * down_rows, down_rows), down_rows)]
+    )
+    place.greet()
+
+    net.wait(cot_moves)
+    for slot in range(slots):
+        dm[span(slot)] = dm[span(slot)] * live_in[slot].astype(BF)
+    net.wait(act_moves)
+
+    chunks = []
+    flights = []
+
+    def advance_zero(k):
+        st, a = chunks[k], k % RING_A
+        st["s0"].wait_recv()
+
+        @pl.loop(0, 4)
+        def _(i):
+            gbuf[a, c, i] = gbuf[a, c, i] + r0[a, i]
+
+        pl.semaphore_signal(free_sems.at[0], inc=1, device_id=place.to_c, device_id_type=MESH)
+        b = k % RING_B
+        if k >= RING_B:
+            pl.semaphore_wait(free_sems.at[1], 1)
+            pl.semaphore_wait(free_sems.at[2], 1)
+        st["s1y"] = net.send(gbuf.at[a, c, pl.ds(0, 2), 1 - y], r1y.at[b], place.to_y)
+        st["s1x"] = net.send(gbuf.at[a, c, 3 - x], r1x.at[b], place.to_x)
+
+    def advance_one(k):
+        st, a, b = chunks[k], k % RING_A, k % RING_B
+        st["s1y"].wait_recv()
+        for i in range(2):
+            gbuf[a, c, i, y] = gbuf[a, c, i, y] + r1y[b, i]
+        st["s2x"] = net.send(gbuf.at[a, c, 1 - x, y], r2x.at[b], place.to_x)
+        st["s1x"].wait_recv()
+        for i in range(2):
+            gbuf[a, c, 2 + x, i] = gbuf[a, c, 2 + x, i] + r1x[b, i]
+        st["s2y"] = net.send(gbuf.at[a, c, 2 + x, 1 - y], r2y.at[b], place.to_y)
+
+    def advance_two(k):
+        st, a, b = chunks[k], k % RING_A, k % RING_B
+        st["s2x"].wait_recv()
+        fbuf[b, :, 0] = gbuf[a, c, x, y] + r2x[b]
+        st["s2y"].wait_recv()
+        fbuf[b, :, 1] = gbuf[a, c, 2 + x, y] + r2y[b]
+        if k >= RING_B:
+            for shift in range(1, shards):
+                pl.semaphore_wait(free_sems.at[2 + shift], 1)
+        st["s3"] = [
+            net.send(fbuf.at[b, (z + shift) % shards], r3.at[b, shift - 1], place.to_z(shift))
+            for shift in range(1, shards)
+        ]
+        for name in ("s0", "s1x", "s1y", "s2x", "s2y"):
+            st[name].wait_send()
+
+    def advance_three(k):
+        st, b = chunks[k], k % RING_B
+        for copy in st["s3"]:
+            copy.wait_recv()
+        total = fbuf[b, z].astype(F32)
+        for shift in range(1, shards):
+            total = total + r3[b, shift - 1].astype(F32)
+        tbuf[b] = total.astype(BF)
+        st["s4"] = net.send(tbuf.at[b], r4.at[b], place.to_x)
+
+    def advance_four(k, total_chunks=12):
+        st, b = chunks[k], k % RING_B
+        st["s4"].wait_recv()
+        out, kind, col = st["out"]
+        for source, at in ((tbuf, x), (r4, 1 - x)):
+            for p in range(2):
+                value = source[b, p].astype(F32)
+                if kind == "cols":
+                    lanes = pl.ds(pl.multiple_of(col + p * 2 * block + at * block, block), block)
+                    out[:, lanes] = value
+                else:
+                    rows = pl.ds(pl.multiple_of((p * 2 + at) * 64, 64), 64)
+                    out[rows, pl.ds(col, block)] = value
+        for copy in st["s3"]:
+            copy.wait_send()
+        st["s4"].wait_send()
+        if k + RING_B < total_chunks:
+            pl.semaphore_signal(free_sems.at[1], inc=1, device_id=place.to_x, device_id_type=MESH)
+            pl.semaphore_signal(free_sems.at[2], inc=1, device_id=place.to_y, device_id_type=MESH)
+            for shift in range(1, shards):
+                peer = {"shard": place.behind(shift)}
+                pl.semaphore_signal(free_sems.at[2 + shift], inc=1, device_id=peer, device_id_type=MESH)
+
+    stages = (advance_zero, advance_one, advance_two, advance_three, advance_four)
+
+    def pump():
+        for flight in flights:
+            if flight[1] < len(stages):
+                stages[flight[1]](flight[0])
+                flight[1] += 1
+
+    def launch(out, kind, col):
+        k = len(chunks)
+        a = k % RING_A
+        if k >= RING_A:
+            pl.semaphore_wait(free_sems.at[0], 1)
+        chunks.append({"out": (out, kind, col)})
+        chunks[k]["s0"] = net.send(gbuf.at[a, 1 - c], r0.at[a], place.to_c)
+        flights.append([k, 0])
+
+    def grad_cols(pairs, out, col):
+        a = len(chunks) % RING_A
+
+        @pl.loop(0, 4)
+        def _(i):
+            total = None
+            for left, right in pairs:
+                term = dot(left[...], right(i), TN)
+                total = term if total is None else total + term
+            value = total.astype(BF).reshape(shards, 2, 2, 64, block)
+            for cc in range(2):
+                for yy in range(2):
+                    gbuf[a, cc, i, yy] = value[:, yy, cc]
+
+        launch(out, "cols", col)
+
+    def grad_down(j):
+        a = len(chunks) % RING_A
+        right = dm[:, pl.ds(j * block, block)]
+
+        @pl.loop(0, shards)
+        def _(i):
+            left = ad[0, :, pl.ds(pl.multiple_of(i * down_rows, down_rows), down_rows)]
+            value = dot(left, right, TN).astype(BF).reshape(2, 2, 4, 64, block)
+            for cc in range(2):
+                for yy in range(2):
+                    gbuf[a, cc, :, yy, i] = value[yy, cc]
+
+        launch(gd, "rows", j * block)
+
+    def lanes_at(start, n=block):
+        return pl.ds(pl.multiple_of(start, block), n)
+
+    grad_down(0)
+    slope_moves = [net.move(slope_in, ad.at[1])]
+    nm_moves = [net.move(nm_in, nm), net.move(res_in, res)]
+    half_rows = width // 2
+    per = half_rows // shard_rows
+    wu_moves = blocks_of(
+        wu_in, wu_all, pl.ds(0, hidden),
+        lambda a: wb.at[a // per, pl.ds(pl.multiple_of((a % per) * shard_rows, shard_rows), shard_rows)],
+    )
+    late_moves = [
+        net.move(att_in, att), net.move(q_in, qv), net.move(normed_in, normed), net.move(x_in, xv),
+        net.move(lse_in, lsev),
+    ]
+    pump()
+    grad_down(1)
+    net.wait(wd_moves)
+    net.wait(slope_moves)
+    wide = 512
+
+    def d_pre(lo, hi):
+        @pl.loop(lo, hi)
+        def _(j):
+            lanes = pl.ds(pl.multiple_of(j * wide, wide), wide)
+            value = dot(dm[...], wa[lanes, :], NT) * ad[1, :, lanes].astype(F32)
+            value = value.astype(BF)
+            ad[1, :, lanes] = value
+            ub[j] = col_sum(value)
+
+    n_wide = hidden // wide
+    d_pre(0, n_wide // 2)
+    pump()
+    grad_down(2)
+    d_pre(n_wide // 2, n_wide)
+    pump()
+    grad_down(3)
+
+    def full(row):
+        return jnp.concatenate([small_in[s, row : row + 1] for s in range(shards)], axis=1).astype(F32)
+
+    net.wait(nm_moves)
+    down_bias = full(7)
+    for slot in range(slots):
+        value = res[span(slot)] + dot(ad[0, span(slot)], wa[...]) + down_bias
+        value = (value * live_in[slot]).astype(BF)
+        dbr[span(slot)] = value
+    layer_moves = [net.move(dbr.at[span(slot)], layer_out.at[slot]) for slot in range(slots)]
+    sg[7:8] = col_sum(dm[...])
+    pump()
+
+    kv_moves = [net.move(kv_in, wa)]
+    wo_moves = []
+    for s in range(shards):
+        at = place.behind(s)
+        src = wo_in if s == 0 else wo_all.at[s]
+        rows = pl.ds(pl.multiple_of((at % per) * shard_rows, shard_rows), shard_rows)
+        wo_moves.append(net.move(src, ad.at[0, rows, pl.ds(pl.multiple_of((at // per) * width, width), width)]))
+
+    def up_pairs(j):
+        return [(nm, lambda i: ad[1, :, lanes_at(j * width + i * block)])]
+
+    grad_cols(up_pairs(0), gu, 0)
+    net.wait(wu_moves)
+    net.wait(layer_moves)
+    gain = full(5)
+    gain_terms, shift_terms = None, None
+    for slot in range(slots):
+        rows = span(slot)
+        incoming = jnp.concatenate([dot(ad[1, rows], wb[i], NT) for i in range(2)], axis=1)
+        back, terms = norm_back(res[rows], gain, incoming)
+        back = back + dm[rows].astype(F32)
+        res[rows] = back
+        dbr[rows] = back.astype(BF)
+        terms, shifts = col_sum(terms), col_sum(incoming)
+        gain_terms = terms if slot == 0 else gain_terms + terms
+        shift_terms = shifts if slot == 0 else shift_terms + shifts
+    sg[5:6] = gain_terms
+    sg[6:7] = shift_terms
+    sg[4:5] = col_sum(dbr[...])
+    pump()
+    grad_cols(up_pairs(1), gu, width)
+    net.wait(wo_moves)
+    for i in range(2):
+        dm[:, i * half_rows : (i + 1) * half_rows] = dot(
+            dbr[...], ad[0, :, i * width : (i + 1) * width], NT
+        ).astype(BF)
+    pl.semaphore_signal(act_free, inc=1, device_id=place.to_c, device_id_type=MESH)
+    pump()
+    grad_cols(up_pairs(2), gu, 2 * width)
+    net.wait(late_moves)
+    net.wait(kv_moves)
+    scale = HEAD_DIM**-0.5
+
+    def attend(slot, lo, hi):
+        masks = head_masks(length)
+
+        @pl.loop(lo, hi)
+        def _(p):
+            lanes = pl.ds(pl.multiple_of(p * PAIR, PAIR), PAIR)
+            rows = span(slot)
+            keys = wa[pl.ds(slot * 2 * clip, clip), lanes]
+            values = wa[pl.ds((slot * 2 + 1) * clip, clip), lanes]
+            queries = qv[rows, lanes] * BF(scale)
+            d_out = dm[rows, lanes]
+            along = (att[rows, lanes].astype(F32) * d_out.astype(F32)).T
+            logs = lsev[slot, p]
+            d_k, d_v, d_q = None, None, []
+            for h in range(2):
+                half = slice(h * HEAD_DIM, (h + 1) * HEAD_DIM)
+                q_h, d_h = queries * masks[h], d_out * masks[h]
+                probs = jnp.exp(dot(keys, q_h, NT) - logs[:, h * length : (h + 1) * length])
+                mean = jnp.sum(along[half], axis=0, keepdims=True)
+                d_scores = (probs * (dot(values, d_h, NT) - mean)).astype(BF)
+                term_v = dot(probs.astype(BF), d_h)
+                term_k = dot(d_scores, q_h)
+                d_v = term_v if h == 0 else d_v + term_v
+                d_k = term_k if h == 0 else d_k + term_k
+                d_q.append(dot(keys, d_scores, TN)[half])
+            qv[rows, lanes] = (jnp.concatenate(d_q, axis=0).T * scale).astype(BF)
+            for part, value in ((0, d_k), (1, d_v)):
+                value = value.astype(BF)
+                for yy in range(2):
+                    to = pl.ds(pl.multiple_of((yy * 2 + part) * width + p * PAIR, PAIR), PAIR)
+                    for cc in range(2):
+                        at = (yy * 2 + cc) * length
+                        wb[cc, rows, to] = value[at : at + length]
+
+    pairs = width // PAIR
+
+    def share(slot):
+        if slot == 0:
+            pl.semaphore_wait(act_free, 1)
+        return net.send(wb.at[1 - c, span(slot)], ad.at[0, span(slot)], place.to_c)
+
+    attend(0, 0, pairs // 2)
+    pump()
+    grad_cols(up_pairs(3), gu, 3 * width)
+    attend(0, pairs // 2, pairs)
+    shares = [share(0)]
+    pump()
+    grad_cols([(att, lambda i: dbr[:, lanes_at(i * block)])], go, 0)
+    attend(1, 0, pairs // 2)
+    pump()
+    attend(1, pairs // 2, pairs)
+    shares.append(share(1))
+    wq_moves = []
+    for part in (1, 2, 0):
+        wq_moves.append(
+            blocks_of(
+                wq_in, wq_all, pl.ds(part * width, width),
+                lambda a: wa.at[pl.ds(pl.multiple_of(part * width + a * shard_rows, shard_rows), shard_rows)],
+            )
+        )
+    pump()
+    grad_cols([(normed.at[0], lambda i: qv[:, lanes_at(i * block)])], gq, 0)
+    sg[2:3] = col_sum(qv[...])
+
+    for slot in range(slots):
+        shares[slot].wait_recv()
+
+        @pl.loop(0, 2 * 2)
+        def _(i):
+            lanes = pl.ds(pl.multiple_of(i * width, width), width)
+            wb[c, span(slot), lanes] = wb[c, span(slot), lanes] + ad[0, span(slot), lanes]
+
+    def d_part(part, which, lanes_from=0, n=None):
+        side = y if which == 0 else 1 - y
+        n = width if n is None else n
+        return wb[c, :, lanes_at((side * 2 + part) * width + lanes_from, n)]
+
+    net.wait(wq_moves[0])
+    net.wait(wq_moves[1])
+    back = dot(d_part(0, 1), wa[pl.ds(width, width)], NT) + dot(d_part(1, 1), wa[pl.ds(2 * width, width)], NT)
+    dm[...] = back.astype(BF)
+    back_sends = [net.send(dm.at[span(slot)], dn.at[slot], place.to_y) for slot in range(slots)]
+    pump()
+
+    def kv_pairs(part):
+        return [
+            (normed.at[which], lambda i, which=which: d_part(part, which, i * block, block)) for which in range(2)
+        ]
+
+    grad_cols(kv_pairs(0), gq, width)
+    sg[3:4] = col_sum(d_part(1, 0)) + col_sum(d_part(1, 1))
+    pump()
+    grad_cols(kv_pairs(1), gq, 2 * width)
+    pump()
+    net.wait(wq_moves[2])
+    gain = full(0)
+    for slot in range(slots):
+        rows = span(slot)
+        incoming = dot(qv[rows], wa[pl.ds(0, width)], NT)
+        side = [wb[c, rows, lanes_at((y * 2 + part) * width, width)] for part in range(2)]
+        incoming = incoming + dot(side[0], wa[pl.ds(width, width)], NT)
+        incoming = incoming + dot(side[1], wa[pl.ds(2 * width, width)], NT)
+        back_sends[slot].wait_recv()
+        incoming = incoming + dn[slot].astype(F32)
+        back, terms = norm_back(xv[slot].astype(F32), gain, incoming)
+        xv[slot] = (res[rows] + back).astype(BF)
+        terms, shifts = col_sum(terms), col_sum(incoming)
+        gain_terms = terms if slot == 0 else gain_terms + terms
+        shift_terms = shifts if slot == 0 else shift_terms + shifts
+        if slot == 0:
+            pump()
+    out_moves = [net.move(xv, input_out)]
+    sg[0:1] = gain_terms
+    sg[1:2] = shift_terms
+    per_row = width // wide
+    for j in range(n_wide):
+        sg[8 + j // per_row : 9 + j // per_row, (j % per_row) * wide : (j % per_row + 1) * wide] = ub[j]
+    sg[12:16] = jnp.zeros((4, width), F32)
+
+    sums = [net.send(sg, sr.at[0], place.to_c)]
+    pump()
+    sums[0].wait_recv()
+    sr[4] = sg[...] + sr[0]
+    sums.append(net.send(sr.at[4], sr.at[1], place.to_y))
+    pump()
+    sums[1].wait_recv()
+    sr[5] = sr[4] + sr[1]
+    sums += [net.send(sr.at[5], sr.at[7 + shift], place.to_z(shift)) for shift in range(1, shards)]
+    pump()
+    for copy in sums[2:]:
+        copy.wait_recv()
+    total = sr[5]
+    for shift in range(1, shards):
+        total = total + sr[7 + shift]
+    sr[6] = total
+    sums.append(net.send(sr.at[6], sr.at[2], place.to_x))
+    pump()
+    sums[-1].wait_recv()
+    sr[3] = sr[6] + sr[2]
+    out_moves.append(net.move(sr.at[3], sg_out))
+    while any(flight[1] < len(stages) for flight in flights):
+        pump()
+    for _ in range(RING_A):
+        pl.semaphore_wait(free_sems.at[0], 1)
+    out_moves += [net.move(a, b) for a, b in ((gq, gq_out), (go, go_out), (gu, gu_out), (gd, gd_out))]
+    finish(net, chunks)
+
+
+def finish(net, chunks):
+    done = set()
+    for st in chunks:
+        for name, value in st.items():
+            if name.startswith("s"):
+                done.update(id(copy) for copy in (value if isinstance(value, list) else [value]))
+    for copy in net.remote:
+        if id(copy) not in done:
+            copy.wait_send()
+    net.wait(net.local)
+
+
+def backward(shards, x, cot, live, small, weights, gathered, kept):
+    slots, length, width = x.shape
+    tokens = slots * length
+    hidden = weights[2].shape[1]
+    down_rows = weights[3].shape[0]
+    pairs = width // PAIR
+    owned = weights[0].shape[0] // 4
+    any_ = pl.BlockSpec(memory_space=pl.ANY)
+    vmem = pl.BlockSpec(memory_space=pltpu.VMEM)
+    sd = jax.ShapeDtypeStruct
+    outs = (
+        sd((slots, length, width), BF), sd((slots, length, width), BF), sd((owned, 3 * width), F32), sd((owned, width), F32),
+        sd((owned, hidden), F32), sd((down_rows // 4, width), F32), sd((16, width), F32),
+    )
+    tile = (64, 256)
+    return pl.pallas_call(
+        functools.partial(backward_kernel, shards),
+        out_shape=outs,
+        in_specs=[any_] * 2 + [vmem] * 2 + [any_] * 17,
+        out_specs=(any_,) * len(outs),
+        scratch_shapes=[
+            pltpu.VMEM((hidden, width), BF),
+            pltpu.VMEM((2, width // 2, hidden), BF),
+            pltpu.VMEM((2, tokens, hidden), BF),
+            pltpu.VMEM((tokens, width), BF),
+            pltpu.VMEM((tokens, width), BF),
+            pltpu.VMEM((tokens, width), F32),
+            pltpu.VMEM((tokens, width), BF),
+            pltpu.VMEM((tokens, width), BF),
+            pltpu.VMEM((tokens, width), BF),
+            pltpu.VMEM((2, tokens, width), BF),
+            pltpu.VMEM((slots, length, width), BF),
+            pltpu.VMEM((slots, length, width), BF),
+            pltpu.VMEM((slots, pairs, 1, 2 * length), F32),
+            pltpu.VMEM((owned, 3 * width), F32),
+            pltpu.VMEM((owned, width), F32),
+            pltpu.VMEM((owned, hidden), F32),
+            pltpu.VMEM((down_rows // 4, width), F32),
+            pltpu.VMEM((16, width), F32),
+            pltpu.VMEM((hidden // 512, 1, 512), F32),
+            pltpu.VMEM((7 + shards, 16, width), F32),
+            pltpu.VMEM((RING_A, 2, 4, 2, shards) + tile, BF),
+            pltpu.VMEM((RING_A, 4, 2, shards) + tile, BF),
+            pltpu.VMEM((RING_B, 2, shards) + tile, BF),
+            pltpu.VMEM((RING_B, 2, shards) + tile, BF),
+            pltpu.VMEM((RING_B, shards) + tile, BF),
+            pltpu.VMEM((RING_B, shards) + tile, BF),
+            pltpu.VMEM((RING_B, shards - 1, 2) + tile, BF),
+            pltpu.VMEM((RING_B, 2) + tile, BF),
+            pltpu.VMEM((RING_B, shards, 2) + tile, BF),
+            pltpu.VMEM((RING_B, 2) + tile, BF),
+            pltpu.SemaphoreType.DMA((N_REMOTE2,)),
+            pltpu.SemaphoreType.DMA((N_REMOTE2,)),
+            pltpu.SemaphoreType.DMA((N_LOCAL2,)),
+            pltpu.SemaphoreType.REGULAR((2 + shards,)),
+            pltpu.SemaphoreType.REGULAR,
+        ],
+        compiler_params=pltpu.CompilerParams(collective_id=2, has_side_effects=True, vmem_limit_bytes=63 * MIB),
+    )(x, cot, live, small, *weights, *gathered, *kept)
 
 
 def local(
     activations, cotangent, clip_loads, attn_gain, attn_shift, w_qkv, q_bias, v_bias, w_out, out_bias,
     mlp_gain, mlp_shift, w_up, up_bias, w_down, down_bias,
 ):
-    shards = lax.axis_size("shard")
-    z = lax.axis_index("shard")
-    x = activations[0]
+    shards, seats = lax.axis_size("shard"), lax.axis_size("seq")
+    x, cot = activations[0], cotangent[0]
     slots, length, width = x.shape
-    tokens = slots * length
-    heads = width // HEAD_DIM
     rows = w_qkv.shape[0]
     vectors = [attn_gain, attn_shift, q_bias, v_bias, out_bias, mlp_gain, mlp_shift, down_bias]
     small = jnp.concatenate([jnp.stack(vectors), up_bias.reshape(-1, rows)], axis=0)
     small = jnp.pad(small, ((0, 16 - small.shape[0]), (0, 0)))
-    (wq, wo, wu, wd, normed, q, kv, lse, att, res, nm, act, slope, smalls) = forward(
-        shards, x, small, w_qkv, w_out, w_up, w_down
-    )
-    order = (z - jnp.arange(shards)) % shards
-
-    def whole(gathered, own):
-        return gathered.at[0].set(own)[order].reshape((-1,) + own.shape[1:])
-
-    wq, wo, wu, wd = whole(wq, w_qkv), whole(wo, w_out), whole(wu, w_up), whole(wd, w_down)
-    full = jnp.concatenate([smalls[s] for s in range(shards)], axis=1).astype(F32)
-    live = (jnp.arange(slots) < clip_loads[0]).astype(F32)[:, None, None]
-    live = jnp.broadcast_to(live, (slots, length, 1)).reshape(tokens, 1)
-    out_grad = cotangent[0].reshape(tokens, width).astype(F32) * live
-    layer_out = (live * (res + jnp.dot(act, wd, preferred_element_type=F32) + full[7:8])).astype(BF)
-    d_mlp = out_grad.astype(BF)
-    grad_w_down = contract_rows(act, d_mlp)
-    grad_down_bias = row_total(d_mlp)
-    d_pre = (contract_cols(d_mlp, wd) * slope.astype(F32)).astype(BF)
-    grad_w_up = contract_rows(nm, d_pre)
-    grad_up_bias = row_total(d_pre)
-    d_norm = contract_cols(d_pre, wu)
-    d_res_norm, grad_mlp_gain, grad_mlp_shift = norm_pull(res, full[5], full[6], d_norm)
-    d_residual = out_grad + d_res_norm
-    d_branch = d_residual.astype(BF)
-    grad_w_out = contract_rows(att, d_branch)
-    grad_out_bias = row_total(d_branch)
-    d_att = contract_cols(d_branch, wo).astype(BF)
-    scale = HEAD_DIM**-0.5
-    d_q, d_kv = [], []
-    for slot in range(slots):
-        span = slice(slot * length, (slot + 1) * length)
-        queries = q[span].reshape(length, heads, HEAD_DIM)
-        keys = kv[slot, :, :, :width].reshape(-1, heads, HEAD_DIM)
-        values = kv[slot, :, :, width:].reshape(-1, heads, HEAD_DIM)
-        d_a = d_att[span].reshape(length, heads, HEAD_DIM)
-        logs = lse[slot].reshape(heads, length)
-        scores = jnp.einsum("thd,lhd->htl", queries, keys, preferred_element_type=F32) * scale
-        probs = jnp.exp(scores - logs[:, :, None])
-        d_probs = jnp.einsum("thd,lhd->htl", d_a, values, preferred_element_type=F32)
-        d_scores = (probs * (d_probs - jnp.sum(probs * d_probs, axis=-1, keepdims=True))).astype(BF)
-        d_q.append(jnp.einsum("htl,lhd->thd", d_scores, keys, preferred_element_type=F32).reshape(length, width) * scale)
-        d_k = jnp.einsum("htl,thd->lhd", d_scores, queries, preferred_element_type=F32) * scale
-        d_v = jnp.einsum("htl,thd->lhd", probs.astype(BF), d_a, preferred_element_type=F32)
-        d_kv.append(jnp.concatenate([d_k.reshape(-1, width), d_v.reshape(-1, width)], axis=1).astype(BF))
-    d_q = jnp.concatenate(d_q).astype(BF)
-    d_kv = jnp.stack(d_kv).reshape(slots, 4, length, 2 * width)
-    d_kv = lax.psum_scatter(d_kv, "seq", scatter_dimension=1, tiled=True).reshape(tokens, 2 * width)
-    d_project = jnp.concatenate([d_q, d_kv], axis=1)
-    grad_w_qkv = contract_rows(normed[0], d_project)
-    grad_q_bias = row_total(d_q)
-    grad_v_bias = row_total(d_kv[:, width:])
-    d_norm1 = contract_cols(d_project, wq)
-    d_in, grad_attn_gain, grad_attn_shift = norm_pull(x.reshape(tokens, width).astype(F32), full[0], full[1], d_norm1)
-    input_grad = (d_residual + d_in).astype(BF)
-
-    def scatter(value):
-        value = lax.psum_scatter(value.astype(BF), ("shard", "seq"), scatter_dimension=0, tiled=True)
-        return lax.psum(value, "replica").astype(F32)
-
-    def total(value):
-        value = lax.psum(value, ("replica", "shard", "seq"))
-        n = value.shape[0] // (shards * lax.axis_size("seq"))
-        at = z * lax.axis_size("seq") + lax.axis_index("seq")
-        return lax.dynamic_slice_in_dim(value, at * n, n)
-
-    shape = activations.shape
+    weights = (w_qkv, w_out, w_up, w_down)
+    *gathered, normed, q, kv, lse, att, res, nm, act, slope, small = forward(shards, x, small, *weights)
+    live = (jnp.arange(slots) < clip_loads[0]).astype(F32)
+    live = jnp.broadcast_to(live[:, None, None], (slots, 1, width))
+    kept = (normed, q, kv.reshape(-1, width), lse, att, res, nm, act, slope)
+    layer_out, input_grad, gq, go, gu, gd, sums = backward(shards, x, cot, live, small, weights, gathered, kept)
+    pods = lax.axis_size("replica")
+    if pods > 2:
+        ends = [[p for p in range(pods) if p % 2 == side] for side in range(2)]
+        gq, go, gu, gd = (
+            lax.psum(g.astype(BF), "replica", axis_index_groups=ends).astype(F32) for g in (gq, go, gu, gd)
+        )
+        sums = lax.psum(sums, "replica", axis_index_groups=ends)
+    at = lax.axis_index("shard") * seats + lax.axis_index("seq")
+    n = width // (shards * seats)
+    vec = lax.dynamic_slice_in_dim(sums[:8], at * n, n, axis=1)
+    n_up = n * 4
+    up = lax.dynamic_slice_in_dim(sums[8:12].reshape(-1), at * n_up, n_up)
     return (
-        layer_out.reshape(shape), input_grad.reshape(shape), total(grad_attn_gain), total(grad_attn_shift),
-        scatter(grad_w_qkv), total(grad_q_bias), total(grad_v_bias), scatter(grad_w_out), total(grad_out_bias),
-        total(grad_mlp_gain), total(grad_mlp_shift), scatter(grad_w_up), total(grad_up_bias),
-        scatter(grad_w_down), total(grad_down_bias),
+        layer_out[None], input_grad[None], vec[0], vec[1], gq, vec[2], vec[3], go, vec[4], vec[5], vec[6], gu, up, gd, vec[7],
     )
 
 

time: 896 us -> 323 us (0.36)
  waiting for transfers between devices: 371 us -> 0 us
  Pallas kernels: 121 us -> 297 us
  local copies, waits for them, and re-layouts: 158 us -> 18.4 us
  matrix products: 123 us -> 0 us
  other arithmetic: 57.4 us -> 0.01 us
  blocking collectives: 41.6 us -> 0 us
  between operations: 15.7 us -> 1.8 us
    reduce_scatter x5 -> x0, waiting for transfers between devices: 371 us -> none  [the longest x4 331 us: scatter(): lax.psum_scatter(value.astype(BF), ('shard', 'seq'), scatter_dimension=0,...]
    pallas_call x0 -> x1, Pallas kernels: none -> 177 us  [backward(): pl.pallas_call(functools.partial(backward_kernel, shards), out_shape=outs...]
    dot_general x19 -> x0, matrix products: 123 us -> none  [the longest x4 28.4 us: contract_rows(): return lax.dot_general(left, right, TN, preferred_element_type=F32)]
    gather x8 -> x0, local copies, waits for them, and re-layouts: 42.4 us -> none  [whole(): return gathered.at[0].set(own)[order].reshape((-1,) + own.shape[1:])]
    psum x1 -> x0, blocking collectives: 41.6 us -> none  [total(): value = lax.psum(value, ('replica', 'shard', 'seq'))]
    concatenate x8 -> x0, local copies, waits for them, and re-layouts: 29 us -> none  [local(): jnp.concatenate([d_k.reshape(-1, width), d_v.reshape(-1, width)], axis=1)]
    convert_element_type x9 -> x1, other arithmetic: 26.4 us -> 0.01 us  [local(): live = (jnp.arange(slots) < clip_loads[0]).astype(F32)]
    slice x12 -> x1, local copies, waits for them, and re-layouts: 26.7 us -> 0.91 us  [local(): vec = lax.dynamic_slice_in_dim(sums[:8], at * n, n, axis=1)]
  transfers between devices with their start and end apart: 6 -> 0, of which waited for: 5 -> 0; matrix products, arithmetic and copies ran while one was open for 10% -> 0% of each run, Pallas kernels for 0% -> 0%
where the time goes in v2:
time: 323 us; the launch traced here: 317 us
  Pallas kernels  297 us (92%)
  local copies, waits for them, and re-layouts  18.4 us (6%)
    pallas_call x1, Pallas kernels, backward(): pl.pallas_call(functools.partial(backward_kernel, shards), out_shape=outs...  177 us
    pallas_call x1, Pallas kernels, forward(): pl.pallas_call(functools.partial(forward_kernel, shards), out_shape=outs,...  121 us
    unnamed x16, local copies, waits for them, and re-layouts  8.92 us

profile of v2, /device:TPU:0, one launch (start us, length us, event | category | flops | bytes accessed | tf_op | source)
XLA Modules:
  0.0 317.4 jit_solution(14061307312459529123)
XLA Ops:
  0.6 0.7 reshape.46
  1.3 0.7 stack.24
  2.0 0.7 stack.25
  2.7 0.7 stack.26
  3.3 0.7 stack.27
  4.0 0.7 stack.28
  4.6 0.7 stack.29
  5.3 0.7 stack.30
  5.9 0.7 stack.31
  6.7 0.6 pad.4.small_in
  7.3 120.6 %shard_map.271 = (bf16[4,256,3072]{2,1,0:T(8,128)(2,1)}, bf16[4,256,1024]{2,1,0:T(8,128)(2,1)}, bf16[4,256,4096]{2,1,0:T(8,128)(2,1)}, bf16[4,1024,1024]{2,1,0:T...) custom-call(bf16[2,256,1024]{2,1,0:T(8,128)(2,1)} %bitcast.29, ...), custom_call_target="tpu_custom_call" | custom-call | tf_op jit(solution)/shard_map/pallas_call | solution.py:374
  128.5 0.7 broadcast_in_dim.12.live_in
  129.2 176.6 %shard_map.272 = (bf16[2,256,1024]{2,1,0:T(8,128)(2,1)}, bf16[2,256,1024]{2,1,0:T(8,128)(2,1)}, f32[64,3072]{1,0:T(8,128)}, f32[64,1024]{1,0:T(8,128)}, f32[64,4...) custom-call(bf16[2,256,1024]{2,1,0:T(8,128)(2,1)} %bitcast.30, bf16[2,256,1024]{2,1,0:T(8,128)(2,1)} %bitcast.31, ...), custom_call_target="tpu_custom_call" | custom-call | tf_op jit(solution)/shard_map/pallas_call | solution.py:861
  305.8 0.9 slice.30
  306.7 0.1 constant_dynamic-slice_fusion
  306.8 0.5 slice_bitcast_fusion.1
  307.4 0.8 slice_bitcast_fusion
  308.1 0.6 dynamic_slice.7
  308.8 2.4 copy.41
  311.1 2.3 copy.42
  313.4 0.9 copy.43
  314.3 0.7 copy.44
  315.0 1.0 copy.45
  315.9 1.0 copy.46
  (11 shorter events, 0.1 us)
Async XLA Ops:
  305.8 7.6 %copy-start.2 = (f32[64,3072]{1,0:T(8,128)S(1)}, f32[64,3072]{1,0:T(8,128)}, u32[]{:S(2)}) copy-start(f32[64,3072]{1,0:T(8,128)} %get-tuple-element.84) | copy-start | bytes 2359300
  305.8 8.4 %copy-start.3 = (f32[64,1024]{1,0:T(8,128)S(1)}, f32[64,1024]{1,0:T(8,128)}, u32[]{:S(2)}) copy-start(f32[64,1024]{1,0:T(8,128)} %get-tuple-element.87) | copy-start | bytes 786436
  305.8 9.1 %copy-start.1 = (f32[64,4096]{1,0:T(8,128)S(1)}, f32[64,4096]{1,0:T(8,128)}, u32[]{:S(2)}) copy-start(f32[64,4096]{1,0:T(8,128)} %get-tuple-element.91) | copy-start | bytes 3145732
  308.8 7.2 %copy-start = (f32[256,1024]{1,0:T(8,128)S(1)}, f32[256,1024]{1,0:T(8,128)}, u32[]{:S(2)}) copy-start(f32[256,1024]{1,0:T(8,128)} %get-tuple-element.93) | copy-start | bytes 3145732

commit v3 on v2

--- a/solution.py
+++ b/solution.py
@@ -97,7 +97,9 @@
     return jnp.concatenate([values * masks[0], values * masks[1]], axis=0)
 
 
-N_REMOTE1, N_LOCAL1 = 128, 80
+N_REMOTE1, N_LOCAL1 = 176, 80
+AHEAD = 2
+IN_HALVES = (3, 5, 7)
 
 
 def forward_kernel(
@@ -120,84 +122,94 @@
     small_moves = [net.move(small_in, smv.at[z])]
     small_sends = [net.send(small_in, smv.at[z], place.to_z(s)) for s in range(1, shards)]
     x_moves = [net.move(x_in, xv.at[0])]
-    x_send = net.send(x_in, xv.at[1], place.to_y)
-
-    def piece_rows(chunk, px, py, pc, lo=0, n=None):
-        _, _, _, _, piece, rows, at = chunk
-        n = rows if n is None else n
-        return pl.ds(pl.multiple_of(((px * 2 + py) * 2 + pc) * piece + at + lo, 16), n)
-
-    half = hidden // 2
-    p32, pdn = shard_rows // 8, wd_in.shape[0] // 8
-    chunks = [
-        (wq_in, wq_all, width, width, p32, p32, 0),
-        (wq_in, wq_all, 2 * width, width, p32, p32, 0),
-        (wq_in, wq_all, 0, width, p32, p32, 0),
-        (wo_in, wo_all, 0, width, p32, p32, 0),
-        (wu_in, wu_all, 0, half, p32, p32, 0),
-        (wu_in, wu_all, half, half, p32, p32, 0),
-        (wd_in, wd_all, 0, width, pdn, pdn // 2, 0),
-        (wd_in, wd_all, 0, width, pdn, pdn // 2, pdn // 2),
-    ]
+    x_sends = [net.send(x_in.at[0], xv.at[1, 0], place.to_y)]
+
+    chunks = [(wq_in, wq_all, part * width, 0, False) for part in (1, 2, 0)]
+    chunks.append((wo_in, wo_all, 0, 0, False))
+    chunks += [(wu_in, wu_all, j * width, 0, False) for j in range(hidden // width)]
+    chunks += [(wd_in, wd_all, 0, j * shard_rows, True) for j in range(wd_in.shape[0] // shard_rows)]
+    chunks = [chunk[:4] + (chunk[4] or i in IN_HALVES,) for i, chunk in enumerate(chunks)]
     state = [dict() for _ in chunks]
     others = pl.ds(1, shards - 1)
+    eighth, quarter = shard_rows // 8, shard_rows // 4
+    near, far = {"shard": z + 1 - 2 * (z % 2)}, {"shard": z + 2 - 4 * (z // 2)}
+    at_near = 1 + 2 * (z % 2)
+
+    def region(i, px, py, pc, side=None):
+        _, _, col, row, halves = chunks[i]
+        if halves:
+            h = (px + py) % 2
+            at, n = {None: (0, 2 * quarter), "x": (0, quarter), "y": (quarter, quarter)}[side]
+            rows = pl.ds(pl.multiple_of(row + pc * 2 * quarter + at, 16), n)
+            return rows, pl.ds(pl.multiple_of(col + h * (width // 2), 128), width // 2)
+        cut = width // 4
+        at, n = {None: (0, width), "y": (0, cut), "x": (cut, width - cut)}[side]
+        rows = pl.ds(pl.multiple_of(row + ((px * 2 + py) * 2 + pc) * eighth, 16), eighth)
+        return rows, pl.ds(col + at, n)
 
     def start_z(i):
-        src, all_, col, cols, *_ = ch = chunks[i]
-        rows = piece_rows(ch, x, y, c)
-        cs = pl.ds(col, cols)
-        state[i]["z"] = [
-            net.send(src.at[rows, cs], all_.at[s, rows, cs], place.to_z(s)) for s in range(1, shards)
-        ]
-
-    def pass_piece(i, px, py, pc, lo, n, peer):
-        _, all_, col, cols, *_ = ch = chunks[i]
-        ref = all_.at[others, piece_rows(ch, px, py, pc, lo, n), pl.ds(col, cols)]
+        src, all_, *_ = chunks[i]
+        at = region(i, x, y, c)
+        state[i]["far"] = net.send(src.at[at], all_.at[(2,) + at], far)
+        state[i]["near"] = net.send(src.at[at], all_.at[(at_near,) + at], near)
+
+    def relay(i):
+        all_ = chunks[i][1]
+        at = region(i, x, y, c)
+        state[i]["far"].wait_recv()
+        state[i]["relay"] = net.send(all_.at[(2,) + at], all_.at[(4 - at_near,) + at], near)
+        if i + AHEAD < len(chunks):
+            start_z(i + AHEAD)
+
+    def pass_piece(i, px, py, pc, peer, side=None):
+        ref = chunks[i][1].at[(others,) + region(i, px, py, pc, side)]
         return net.send(ref, ref, peer)
 
     def plane_one(i):
-        rows = chunks[i][5]
         st = state[i]
-        for copy in st["z"]:
-            copy.wait_recv()
-        st["x"] = pass_piece(i, x, y, c, 0, rows, place.to_x)
-        st["y"] = pass_piece(i, x, y, c, 0, rows, place.to_y)
-        st["core"] = [pass_piece(i, x, y, c, 0, rows, place.to_c)]
+        st["near"].wait_recv()
+        st["relay"].wait_recv()
+        halves = chunks[i][4]
+        st["x"] = pass_piece(i, x, y, c, place.to_x, "x" if halves else None)
+        st["y"] = pass_piece(i, x, y, c, place.to_y, "y" if halves else None)
+        st["core"] = [pass_piece(i, x, y, c, place.to_c)]
 
     def plane_two(i):
-        rows = chunks[i][5]
         st = state[i]
+        halves = chunks[i][4]
+        st["y"].wait_recv()
+        if not halves:
+            st["yx"] = pass_piece(i, x, 1 - y, c, place.to_x, "x")
+        st["core"].append(pass_piece(i, x, 1 - y, c, place.to_c, "y" if halves else None))
         st["x"].wait_recv()
-        st["xy"] = pass_piece(i, 1 - x, y, c, 0, rows // 2, place.to_y)
-        st["core"].append(pass_piece(i, 1 - x, y, c, 0, rows, place.to_c))
-        st["y"].wait_recv()
-        st["yx"] = pass_piece(i, x, 1 - y, c, rows // 2, rows // 2, place.to_x)
-        st["core"].append(pass_piece(i, x, 1 - y, c, 0, rows, place.to_c))
+        if not halves:
+            st["xy"] = pass_piece(i, 1 - x, y, c, place.to_y, "y")
+        st["core"].append(pass_piece(i, 1 - x, y, c, place.to_c, "x" if halves else None))
 
     def plane_three(i):
-        rows = chunks[i][5]
         st = state[i]
-        st["xy"].wait_recv()
-        st["core"].append(pass_piece(i, 1 - x, 1 - y, c, 0, rows // 2, place.to_c))
-        st["yx"].wait_recv()
-        st["core"].append(pass_piece(i, 1 - x, 1 - y, c, rows // 2, rows // 2, place.to_c))
+        if chunks[i][4]:
+            return
+        for name, side in (("yx", "x"), ("xy", "y")):
+            st[name].wait_recv()
+            st["core"].append(pass_piece(i, 1 - x, 1 - y, c, place.to_c, side))
 
     def arrived(i):
         for copy in state[i]["core"]:
             copy.wait_recv()
 
     def load(i, dst):
-        src, all_, col, cols, *_ = chunks[i]
+        src, all_, col, *_ = chunks[i]
         moves = []
         for s in range(shards):
             rows = pl.ds(pl.multiple_of(place.behind(s) * shard_rows, shard_rows), shard_rows)
-            cs = pl.ds(col, cols)
+            cs = pl.ds(col, width)
             from_ = src.at[:, cs] if s == 0 else all_.at[s, :, cs]
             moves.append(net.move(from_, dst.at[rows, cs]))
         return moves
 
-    start_z(0)
-    start_z(1)
+    for i in range(AHEAD):
+        start_z(i)
 
     net.wait(small_moves)
     for copy in small_sends:
@@ -207,36 +219,43 @@
     def small(row, count=1):
         return jnp.concatenate([smv[s] for s in range(shards)], axis=1)[row : row + count].astype(F32)
 
-    def norm_first(which):
-        gain, shift = small(0), small(1)
-        for slot in range(slots):
-            rows = pl.ds(slot * length, length)
-            normed[which, rows, :] = normalized(xv[which, slot].astype(F32), gain, shift).astype(BF)
+    def norm_first(which, slot):
+        rows = pl.ds(slot * length, length)
+        normed[which, rows, :] = normalized(xv[which, slot].astype(F32), small(0), small(1)).astype(BF)
+
+    loads = {}
+
+    def step(i):
+        if i + 4 < len(chunks):
+            relay(i + 4)
+        if i + 2 < len(chunks):
+            plane_one(i + 2)
+        if 0 <= i + 1 < len(chunks):
+            plane_two(i + 1)
+        if 0 <= i < len(chunks):
+            plane_three(i)
+        if 0 <= i - 1:
+            arrived(i - 1)
+            if i - 1 < len(targets):
+                loads[i - 1] = load(i - 1, targets[i - 1])
+
+    targets = [wq] * 3 + [wo] + [wu] * (hidden // width)
 
     net.wait(x_moves)
-    norm_first(0)
-    plane_one(0)
-    start_z(2)
-    plane_one(1)
-    plane_two(0)
-    start_z(3)
-    x_send.wait_recv()
-    norm_first(1)
+    norm_first(0, 0)
+    relay(0)
+    relay(1)
+    step(-2)
+    x_sends.append(net.send(x_in.at[1], xv.at[1, 1], place.to_y))
+    norm_first(0, 1)
+    step(-1)
+    x_sends[0].wait_recv()
+    norm_first(1, 0)
+    step(0)
+    x_sends[1].wait_recv()
+    norm_first(1, 1)
     moves_out = [net.move(normed, normed_out)]
-    plane_one(2)
-    plane_two(1)
-    plane_three(0)
-    start_z(4)
-    arrived(0)
-    k_moves = load(0, wq)
-    plane_one(3)
-    plane_two(2)
-    plane_three(1)
-    start_z(5)
-    arrived(1)
-    v_moves = load(1, wq)
-    net.wait(k_moves)
-
+    step(1)
     v_bias = small(3)
 
     def project_kv(which, part):
@@ -258,28 +277,19 @@
             ref = kvb.at[:, part, at]
             shares.append(net.send(ref, ref, place.to_c))
 
+    net.wait(loads[0])
     project_kv(0, 0)
     project_kv(1, 0)
     share(0)
-    plane_one(4)
-    plane_two(3)
-    plane_three(2)
-    start_z(6)
-    arrived(2)
-    q_moves = load(2, wq)
-    net.wait(v_moves)
+    step(2)
+    net.wait(loads[1])
     project_kv(0, 1)
     project_kv(1, 1)
     share(1)
-    plane_three(3)
-    arrived(3)
-    o_moves = load(3, wo)
-    net.wait(q_moves)
+    step(3)
+    net.wait(loads[2])
     qv[...] = (dot(normed[0], wq[:, :width]) + small(2)).astype(BF)
     moves_out.append(net.move(qv, q_out))
-    plane_one(5)
-    plane_two(4)
-    start_z(7)
     for copy in shares:
         copy.wait_recv()
     moves_out.append(net.move(kvb, kv_out))
@@ -304,21 +314,16 @@
             att[rows, lanes] = out.T.astype(BF)
 
     pairs = width // PAIR
-    attend(0, 0, pairs)
-    plane_one(6)
-    plane_two(5)
-    plane_three(4)
-    arrived(4)
-    up_moves = [load(4, wu)]
-    attend(1, 0, pairs)
+    attend(0, 0, pairs // 2)
+    step(4)
+    attend(0, pairs // 2, pairs)
+    step(5)
+    attend(1, 0, pairs // 2)
+    step(6)
+    attend(1, pairs // 2, pairs)
     moves_out += [net.move(lsev, lse_out), net.move(att, att_out)]
-    plane_one(7)
-    plane_two(6)
-    plane_three(5)
-    arrived(5)
-    up_moves.append(load(5, wu))
-
-    net.wait(o_moves)
+    step(7)
+    net.wait(loads[3])
     out_bias, mlp_gain, mlp_shift = small(4), small(5), small(6)
     for slot in range(slots):
         rows = pl.ds(slot * length, length)
@@ -330,7 +335,7 @@
     up_block = 512
 
     def up(part):
-        @pl.loop(part * (half // up_block), (part + 1) * (half // up_block))
+        @pl.loop(part * (width // up_block), (part + 1) * (width // up_block))
         def _(j):
             lanes = pl.ds(pl.multiple_of(j * up_block, up_block), up_block)
             s, inner = j // (wd_in.shape[0] // up_block), j % (wd_in.shape[0] // up_block)
@@ -345,16 +350,16 @@
             act[:, lanes] = (pre * phi).astype(BF)
             slope[:, lanes] = (phi + pre * density).astype(BF)
 
-    net.wait(up_moves[0])
-    up(0)
-    plane_two(7)
-    plane_three(6)
-    net.wait(up_moves[1])
-    up(1)
-    moves_out += [net.move(act, act_out), net.move(slope, slope_out)]
-    plane_three(7)
-    arrived(6)
-    arrived(7)
+    for j in range(hidden // width):
+        if 4 + j not in loads:
+            step(5 + j)
+        net.wait(loads[4 + j])
+        up(j)
+        if j % 2:
+            lanes = pl.ds((j - 1) * width, 2 * width)
+            moves_out += [net.move(act.at[:, lanes], act_out.at[:, lanes]), net.move(slope.at[:, lanes], slope_out.at[:, lanes])]
+    for i in range(9, len(chunks) + 1):
+        step(i)
     net.finish()
 
 
@@ -400,7 +405,8 @@
 
 
 N_REMOTE2, N_LOCAL2 = 160, 80
-RING_A, RING_B = 3, 5
+RING_A, RING_B, N_CHUNKS = 3, 3, 12
+X_ONLY = (8, 9)
 
 
 def norm_back(values, gain, incoming):
@@ -424,7 +430,7 @@
     layer_out, input_out, gq_out, go_out, gu_out, gd_out, sg_out,
     wa, wb, ad, nm, att, res, dm, dbr, qv, normed, xv, dn, lsev,
     gq, go, gu, gd, sg, ub, sr,
-    gbuf, r0, r1x, r1y, r2x, r2y, r3, r4, fbuf, tbuf,
+    gbuf, r0, r1, ra, rb, r2, r4, fbuf, gb, tsum, tbuf,
     send_sems, recv_sems, local_sems, free_sems, act_free,
 ):
     place = Place(shards)
@@ -465,8 +471,14 @@
     chunks = []
     flights = []
 
+    def first_peer(k, p):
+        return place.to_x if p or k in X_ONLY else place.to_y
+
+    def credit(k, p):
+        return free_sems.at[2 if p else 3 if k in X_ONLY else 1]
+
     def advance_zero(k):
-        st, a = chunks[k], k % RING_A
+        st, a, b = chunks[k], k % RING_A, k % RING_B
         st["s0"].wait_recv()
 
         @pl.loop(0, 4)
@@ -474,77 +486,78 @@
             gbuf[a, c, i] = gbuf[a, c, i] + r0[a, i]
 
         pl.semaphore_signal(free_sems.at[0], inc=1, device_id=place.to_c, device_id_type=MESH)
-        b = k % RING_B
-        if k >= RING_B:
-            pl.semaphore_wait(free_sems.at[1], 1)
-            pl.semaphore_wait(free_sems.at[2], 1)
-        st["s1y"] = net.send(gbuf.at[a, c, pl.ds(0, 2), 1 - y], r1y.at[b], place.to_y)
-        st["s1x"] = net.send(gbuf.at[a, c, 3 - x], r1x.at[b], place.to_x)
+        st["s1"] = []
+        for p in range(2):
+            if k >= RING_B:
+                pl.semaphore_wait(credit(k, p), 1)
+            peer = first_peer(k, p)
+            src = gbuf.at[a, c, 2 * p + 1 - x] if peer is place.to_x else gbuf.at[a, c, pl.ds(2 * p, 2), 1 - y]
+            st["s1"].append(net.send(src, r1.at[b, p], peer))
 
     def advance_one(k):
         st, a, b = chunks[k], k % RING_A, k % RING_B
-        st["s1y"].wait_recv()
+        for p in range(2):
+            st["s1"][p].wait_recv()
+            for i in range(2):
+                kept = gbuf[a, c, 2 * p + x, i] if first_peer(k, p) is place.to_x else gbuf[a, c, 2 * p + i, y]
+                value = kept + r1[b, p, i]
+                for zz in range(shards):
+                    fbuf[b, zz % 2, zz // 2, 2 * p + i] = value[zz]
+            if k + RING_B < N_CHUNKS:
+                peer = first_peer(k + RING_B, p)
+                pl.semaphore_signal(credit(k + RING_B, p), inc=1, device_id=peer, device_id_type=MESH)
+        st["sa"] = net.send(fbuf.at[b, 1 - z % 2], ra.at[k], {"shard": z + 1 - 2 * (z % 2)})
+        for copy in [st["s0"]] + st["s1"]:
+            copy.wait_send()
+
+    def advance_two(k):
+        st, b = chunks[k], k % RING_B
+        st["sa"].wait_recv()
         for i in range(2):
-            gbuf[a, c, i, y] = gbuf[a, c, i, y] + r1y[b, i]
-        st["s2x"] = net.send(gbuf.at[a, c, 1 - x, y], r2x.at[b], place.to_x)
-        st["s1x"].wait_recv()
-        for i in range(2):
-            gbuf[a, c, 2 + x, i] = gbuf[a, c, 2 + x, i] + r1x[b, i]
-        st["s2y"] = net.send(gbuf.at[a, c, 2 + x, 1 - y], r2y.at[b], place.to_y)
-
-    def advance_two(k):
-        st, a, b = chunks[k], k % RING_A, k % RING_B
-        st["s2x"].wait_recv()
-        fbuf[b, :, 0] = gbuf[a, c, x, y] + r2x[b]
-        st["s2y"].wait_recv()
-        fbuf[b, :, 1] = gbuf[a, c, 2 + x, y] + r2y[b]
-        if k >= RING_B:
-            for shift in range(1, shards):
-                pl.semaphore_wait(free_sems.at[2 + shift], 1)
-        st["s3"] = [
-            net.send(fbuf.at[b, (z + shift) % shards], r3.at[b, shift - 1], place.to_z(shift))
-            for shift in range(1, shards)
-        ]
-        for name in ("s0", "s1x", "s1y", "s2x", "s2y"):
-            st[name].wait_send()
+            gb[b, i] = fbuf[b, z % 2, i] + ra[k, i]
+        st["sb"] = net.send(gb.at[b, 1 - z // 2], rb.at[k], {"shard": z + 2 - 4 * (z // 2)})
+        st["sa"].wait_send()
 
     def advance_three(k):
         st, b = chunks[k], k % RING_B
-        for copy in st["s3"]:
-            copy.wait_recv()
-        total = fbuf[b, z].astype(F32)
-        for shift in range(1, shards):
-            total = total + r3[b, shift - 1].astype(F32)
-        tbuf[b] = total.astype(BF)
-        st["s4"] = net.send(tbuf.at[b], r4.at[b], place.to_x)
-
-    def advance_four(k, total_chunks=12):
+        st["sb"].wait_recv()
+        tsum[b] = gb[b, z // 2] + rb[k]
+        st["s2"] = []
+        for p in range(2):
+            over_y = first_peer(k, p) is place.to_x
+            src = tsum.at[b, 2 * p + 1 - (y if over_y else x)]
+            st["s2"].append(net.send(src, r2.at[k, p], place.to_y if over_y else place.to_x))
+        st["sb"].wait_send()
+
+    def advance_four(k):
+        st, b = chunks[k], k % RING_B
+        for p in range(2):
+            st["s2"][p].wait_recv()
+            at = y if first_peer(k, p) is place.to_x else x
+            tbuf[b, p] = tsum[b, 2 * p + at] + r2[k, p]
+        st["s4"] = net.send(tbuf.at[b], r4.at[k], place.to_x)
+        for copy in st["s2"]:
+            copy.wait_send()
+
+    def advance_five(k):
         st, b = chunks[k], k % RING_B
         st["s4"].wait_recv()
         out, kind, col = st["out"]
-        for source, at in ((tbuf, x), (r4, 1 - x)):
+        for source, slot, at in ((tbuf, b, x), (r4, k, 1 - x)):
             for p in range(2):
-                value = source[b, p].astype(F32)
+                value = source[slot, p]
                 if kind == "cols":
                     lanes = pl.ds(pl.multiple_of(col + p * 2 * block + at * block, block), block)
                     out[:, lanes] = value
                 else:
                     rows = pl.ds(pl.multiple_of((p * 2 + at) * 64, 64), 64)
                     out[rows, pl.ds(col, block)] = value
-        for copy in st["s3"]:
-            copy.wait_send()
         st["s4"].wait_send()
-        if k + RING_B < total_chunks:
-            pl.semaphore_signal(free_sems.at[1], inc=1, device_id=place.to_x, device_id_type=MESH)
-            pl.semaphore_signal(free_sems.at[2], inc=1, device_id=place.to_y, device_id_type=MESH)
-            for shift in range(1, shards):
-                peer = {"shard": place.behind(shift)}
-                pl.semaphore_signal(free_sems.at[2 + shift], inc=1, device_id=peer, device_id_type=MESH)
-
-    stages = (advance_zero, advance_one, advance_two, advance_three, advance_four)
+
+    stages = (advance_zero, advance_one, advance_two, advance_three, advance_four, advance_five)
 
     def pump():
-        for flight in flights:
+        for flight in reversed(flights):
             if flight[1] < len(stages):
                 stages[flight[1]](flight[0])
                 flight[1] += 1
@@ -591,21 +604,20 @@
     def lanes_at(start, n=block):
         return pl.ds(pl.multiple_of(start, block), n)
 
+    slope_moves = [net.move(slope_in, ad.at[1])]
     grad_down(0)
-    slope_moves = [net.move(slope_in, ad.at[1])]
-    nm_moves = [net.move(nm_in, nm), net.move(res_in, res)]
     half_rows = width // 2
     per = half_rows // shard_rows
     wu_moves = blocks_of(
         wu_in, wu_all, pl.ds(0, hidden),
         lambda a: wb.at[a // per, pl.ds(pl.multiple_of((a % per) * shard_rows, shard_rows), shard_rows)],
     )
-    late_moves = [
-        net.move(att_in, att), net.move(q_in, qv), net.move(normed_in, normed), net.move(x_in, xv),
-        net.move(lse_in, lsev),
-    ]
-    pump()
-    grad_down(1)
+    nm_moves = [net.move(res_in, res), net.move(nm_in, nm)]
+    wo_moves = blocks_of(
+        wo_in, wo_all, every,
+        lambda a: normed.at[a // per, pl.ds(pl.multiple_of((a % per) * shard_rows, shard_rows), shard_rows)],
+    )
+    late_moves = [net.move(att_in, att), net.move(q_in, qv), net.move(lse_in, lsev)]
     net.wait(wd_moves)
     net.wait(slope_moves)
     wide = 512
@@ -619,45 +631,25 @@
             ad[1, :, lanes] = value
             ub[j] = col_sum(value)
 
-    n_wide = hidden // wide
-    d_pre(0, n_wide // 2)
-    pump()
-    grad_down(2)
-    d_pre(n_wide // 2, n_wide)
-    pump()
-    grad_down(3)
-
     def full(row):
         return jnp.concatenate([small_in[s, row : row + 1] for s in range(shards)], axis=1).astype(F32)
 
+    n_wide = hidden // wide
+    d_pre(0, n_wide // 4)
+    pump()
+    grad_down(1)
+    d_pre(n_wide // 4, n_wide)
+    pump()
+    grad_down(2)
+    net.wait(wu_moves)
     net.wait(nm_moves)
     down_bias = full(7)
-    for slot in range(slots):
-        value = res[span(slot)] + dot(ad[0, span(slot)], wa[...]) + down_bias
-        value = (value * live_in[slot]).astype(BF)
-        dbr[span(slot)] = value
-    layer_moves = [net.move(dbr.at[span(slot)], layer_out.at[slot]) for slot in range(slots)]
-    sg[7:8] = col_sum(dm[...])
-    pump()
-
-    kv_moves = [net.move(kv_in, wa)]
-    wo_moves = []
-    for s in range(shards):
-        at = place.behind(s)
-        src = wo_in if s == 0 else wo_all.at[s]
-        rows = pl.ds(pl.multiple_of((at % per) * shard_rows, shard_rows), shard_rows)
-        wo_moves.append(net.move(src, ad.at[0, rows, pl.ds(pl.multiple_of((at // per) * width, width), width)]))
-
-    def up_pairs(j):
-        return [(nm, lambda i: ad[1, :, lanes_at(j * width + i * block)])]
-
-    grad_cols(up_pairs(0), gu, 0)
-    net.wait(wu_moves)
-    net.wait(layer_moves)
     gain = full(5)
     gain_terms, shift_terms = None, None
     for slot in range(slots):
         rows = span(slot)
+        value = res[rows] + dot(ad[0, rows], wa[...]) + down_bias
+        xv[slot] = (value * live_in[slot]).astype(BF)
         incoming = jnp.concatenate([dot(ad[1, rows], wb[i], NT) for i in range(2)], axis=1)
         back, terms = norm_back(res[rows], gain, incoming)
         back = back + dm[rows].astype(F32)
@@ -666,19 +658,28 @@
         terms, shifts = col_sum(terms), col_sum(incoming)
         gain_terms = terms if slot == 0 else gain_terms + terms
         shift_terms = shifts if slot == 0 else shift_terms + shifts
+        if slot == 0:
+            pump()
+            grad_down(3)
+    layer_moves = [net.move(xv, layer_out)]
+    kv_moves = [net.move(kv_in, wa)]
     sg[5:6] = gain_terms
     sg[6:7] = shift_terms
     sg[4:5] = col_sum(dbr[...])
-    pump()
-    grad_cols(up_pairs(1), gu, width)
+    sg[7:8] = col_sum(dm[...])
     net.wait(wo_moves)
     for i in range(2):
-        dm[:, i * half_rows : (i + 1) * half_rows] = dot(
-            dbr[...], ad[0, :, i * width : (i + 1) * width], NT
-        ).astype(BF)
+        dm[:, i * half_rows : (i + 1) * half_rows] = dot(dbr[...], normed[i], NT).astype(BF)
+    normed_moves = [net.move(normed_in, normed)]
     pl.semaphore_signal(act_free, inc=1, device_id=place.to_c, device_id_type=MESH)
-    pump()
-    grad_cols(up_pairs(2), gu, 2 * width)
+
+    def up_pairs(j):
+        return [(nm, lambda i: ad[1, :, lanes_at(j * width + i * block)])]
+
+    pump()
+    grad_cols(up_pairs(0), gu, 0)
+    net.wait(layer_moves)
+    late_moves.append(net.move(x_in, xv))
     net.wait(late_moves)
     net.wait(kv_moves)
     scale = HEAD_DIM**-0.5
@@ -726,13 +727,14 @@
 
     attend(0, 0, pairs // 2)
     pump()
-    grad_cols(up_pairs(3), gu, 3 * width)
+    grad_cols(up_pairs(1), gu, width)
     attend(0, pairs // 2, pairs)
     shares = [share(0)]
     pump()
-    grad_cols([(att, lambda i: dbr[:, lanes_at(i * block)])], go, 0)
+    grad_cols(up_pairs(2), gu, 2 * width)
     attend(1, 0, pairs // 2)
     pump()
+    grad_cols(up_pairs(3), gu, 3 * width)
     attend(1, pairs // 2, pairs)
     shares.append(share(1))
     wq_moves = []
@@ -744,7 +746,7 @@
             )
         )
     pump()
-    grad_cols([(normed.at[0], lambda i: qv[:, lanes_at(i * block)])], gq, 0)
+    grad_cols([(att, lambda i: dbr[:, lanes_at(i * block)])], go, 0)
     sg[2:3] = col_sum(qv[...])
 
     for slot in range(slots):
@@ -766,6 +768,10 @@
     dm[...] = back.astype(BF)
     back_sends = [net.send(dm.at[span(slot)], dn.at[slot], place.to_y) for slot in range(slots)]
     pump()
+    net.wait(normed_moves)
+    grad_cols([(normed.at[0], lambda i: qv[:, lanes_at(i * block)])], gq, 0)
+    sg[3:4] = col_sum(d_part(1, 0)) + col_sum(d_part(1, 1))
+    pump()
 
     def kv_pairs(part):
         return [
@@ -773,7 +779,6 @@
         ]
 
     grad_cols(kv_pairs(0), gq, width)
-    sg[3:4] = col_sum(d_part(1, 0)) + col_sum(d_part(1, 1))
     pump()
     grad_cols(kv_pairs(1), gq, 2 * width)
     pump()
@@ -854,8 +859,8 @@
     vmem = pl.BlockSpec(memory_space=pltpu.VMEM)
     sd = jax.ShapeDtypeStruct
     outs = (
-        sd((slots, length, width), BF), sd((slots, length, width), BF), sd((owned, 3 * width), F32), sd((owned, width), F32),
-        sd((owned, hidden), F32), sd((down_rows // 4, width), F32), sd((16, width), F32),
+        sd((slots, length, width), BF), sd((slots, length, width), BF), sd((owned, 3 * width), BF), sd((owned, width), BF),
+        sd((owned, hidden), BF), sd((down_rows // 4, width), BF), sd((16, width), F32),
     )
     tile = (64, 256)
     return pl.pallas_call(
@@ -877,44 +882,89 @@
             pltpu.VMEM((slots, length, width), BF),
             pltpu.VMEM((slots, length, width), BF),
             pltpu.VMEM((slots, pairs, 1, 2 * length), F32),
-            pltpu.VMEM((owned, 3 * width), F32),
-            pltpu.VMEM((owned, width), F32),
-            pltpu.VMEM((owned, hidden), F32),
-            pltpu.VMEM((down_rows // 4, width), F32),
+            pltpu.VMEM((owned, 3 * width), BF),
+            pltpu.VMEM((owned, width), BF),
+            pltpu.VMEM((owned, hidden), BF),
+            pltpu.VMEM((down_rows // 4, width), BF),
             pltpu.VMEM((16, width), F32),
             pltpu.VMEM((hidden // 512, 1, 512), F32),
             pltpu.VMEM((7 + shards, 16, width), F32),
             pltpu.VMEM((RING_A, 2, 4, 2, shards) + tile, BF),
             pltpu.VMEM((RING_A, 4, 2, shards) + tile, BF),
-            pltpu.VMEM((RING_B, 2, shards) + tile, BF),
-            pltpu.VMEM((RING_B, 2, shards) + tile, BF),
-            pltpu.VMEM((RING_B, shards) + tile, BF),
-            pltpu.VMEM((RING_B, shards) + tile, BF),
-            pltpu.VMEM((RING_B, shards - 1, 2) + tile, BF),
-            pltpu.VMEM((RING_B, 2) + tile, BF),
-            pltpu.VMEM((RING_B, shards, 2) + tile, BF),
+            pltpu.VMEM((RING_B, 2, 2, shards) + tile, BF),
+            pltpu.VMEM((N_CHUNKS, 2, 4) + tile, BF),
+            pltpu.VMEM((N_CHUNKS, 4) + tile, BF),
+            pltpu.VMEM((N_CHUNKS, 2) + tile, BF),
+            pltpu.VMEM((N_CHUNKS, 2) + tile, BF),
+            pltpu.VMEM((RING_B, 2, 2, 4) + tile, BF),
+            pltpu.VMEM((RING_B, 2, 4) + tile, BF),
+            pltpu.VMEM((RING_B, 4) + tile, BF),
             pltpu.VMEM((RING_B, 2) + tile, BF),
             pltpu.SemaphoreType.DMA((N_REMOTE2,)),
             pltpu.SemaphoreType.DMA((N_REMOTE2,)),
             pltpu.SemaphoreType.DMA((N_LOCAL2,)),
-            pltpu.SemaphoreType.REGULAR((2 + shards,)),
+            pltpu.SemaphoreType.REGULAR((4,)),
             pltpu.SemaphoreType.REGULAR,
         ],
         compiler_params=pltpu.CompilerParams(collective_id=2, has_side_effects=True, vmem_limit_bytes=63 * MIB),
     )(x, cot, live, small, *weights, *gathered, *kept)
 
 
+def place_kernel(n, *refs):
+    srcs, dsts = refs[: n + 1], refs[n + 1 : 2 * n + 3]
+    small, bufs, wide, sems = refs[2 * n + 3], refs[2 * n + 4 : 3 * n + 4], refs[3 * n + 4 : -1], refs[-1]
+    loads = [pltpu.make_async_copy(src, buf, sems.at[i]) for i, (src, buf) in enumerate(zip(srcs, bufs + (small,)))]
+    for copy in loads:
+        copy.start()
+    stores = []
+    for i in range(n):
+        loads[i].wait()
+        buf = bufs[i]
+        if i >= 2:
+            buf = wide[i - 2]
+            buf[...] = bufs[i][...].astype(F32)
+        stores.append(pltpu.make_async_copy(buf, dsts[i], sems.at[n + 1 + i]))
+        stores[-1].start()
+    loads[n].wait()
+    at = lax.axis_index("shard") * lax.axis_size("seq") + lax.axis_index("seq")
+    vec_out, up_out = dsts[n:]
+    pair = small[0:8, pl.ds(pl.multiple_of(at // 2 * 128, 128), 128)]
+    vec_out[...] = jnp.where(at % 2 == 0, pair[:, :64], pair[:, 64:])
+    up_out[...] = small[pl.ds(8 + at // 4, 1), pl.ds(pl.multiple_of(at % 4 * 256, 256), 256)]
+    for copy in stores:
+        copy.wait()
+
+
+def place_results(sums, *arrays):
+    any_, vmem = pl.BlockSpec(memory_space=pl.ANY), pl.BlockSpec(memory_space=pltpu.VMEM)
+    n = len(arrays)
+    outs = tuple(jax.ShapeDtypeStruct(a.shape, F32 if a.ndim == 2 else BF) for a in arrays)
+    return pl.pallas_call(
+        functools.partial(place_kernel, n),
+        out_shape=outs + (jax.ShapeDtypeStruct((8, 64), F32), jax.ShapeDtypeStruct((1, 256), F32)),
+        in_specs=[any_] * (n + 1),
+        out_specs=(any_,) * n + (vmem, vmem),
+        scratch_shapes=[pltpu.VMEM(sums.shape, F32)]
+        + [pltpu.VMEM(a.shape, BF) for a in arrays]
+        + [pltpu.VMEM(a.shape, F32) for a in arrays[2:]]
+        + [pltpu.SemaphoreType.DMA((2 * n + 1,))],
+        compiler_params=pltpu.CompilerParams(vmem_limit_bytes=60 * MIB),
+    )(*arrays, sums)
+
+
 def local(
     activations, cotangent, clip_loads, attn_gain, attn_shift, w_qkv, q_bias, v_bias, w_out, out_bias,
     mlp_gain, mlp_shift, w_up, up_bias, w_down, down_bias,
 ):
-    shards, seats = lax.axis_size("shard"), lax.axis_size("seq")
+    shards = lax.axis_size("shard")
     x, cot = activations[0], cotangent[0]
     slots, length, width = x.shape
     rows = w_qkv.shape[0]
     vectors = [attn_gain, attn_shift, q_bias, v_bias, out_bias, mlp_gain, mlp_shift, down_bias]
-    small = jnp.concatenate([jnp.stack(vectors), up_bias.reshape(-1, rows)], axis=0)
-    small = jnp.pad(small, ((0, 16 - small.shape[0]), (0, 0)))
+    small = jnp.broadcast_to(up_bias.reshape(1, 4, rows), (4, 4, rows)).reshape(16, rows)
+    row = lax.broadcasted_iota(jnp.int32, (16, rows), 0)
+    for i, vector in enumerate(vectors):
+        small = jnp.where(row == i, vector[None, :], small)
     weights = (w_qkv, w_out, w_up, w_down)
     *gathered, normed, q, kv, lse, att, res, nm, act, slope, small = forward(shards, x, small, *weights)
     live = (jnp.arange(slots) < clip_loads[0]).astype(F32)
@@ -924,17 +974,10 @@
     pods = lax.axis_size("replica")
     if pods > 2:
         ends = [[p for p in range(pods) if p % 2 == side] for side in range(2)]
-        gq, go, gu, gd = (
-            lax.psum(g.astype(BF), "replica", axis_index_groups=ends).astype(F32) for g in (gq, go, gu, gd)
-        )
-        sums = lax.psum(sums, "replica", axis_index_groups=ends)
-    at = lax.axis_index("shard") * seats + lax.axis_index("seq")
-    n = width // (shards * seats)
-    vec = lax.dynamic_slice_in_dim(sums[:8], at * n, n, axis=1)
-    n_up = n * 4
-    up = lax.dynamic_slice_in_dim(sums[8:12].reshape(-1), at * n_up, n_up)
+        gq, go, gu, gd, sums = (lax.psum(g, "replica", axis_index_groups=ends) for g in (gq, go, gu, gd, sums))
+    layer_out, input_grad, gq, go, gu, gd, vec, up = place_results(sums, layer_out, input_grad, gq, go, gu, gd)
     return (
-        layer_out[None], input_grad[None], vec[0], vec[1], gq, vec[2], vec[3], go, vec[4], vec[5], vec[6], gu, up, gd, vec[7],
+        layer_out[None], input_grad[None], vec[0], vec[1], gq, vec[2], vec[3], go, vec[4], vec[5], vec[6], gu, up[0], gd, vec[7],
     )
 
 

time: 323 us -> 282 us (0.87)
  Pallas kernels: 297 us -> 271 us
  local copies, waits for them, and re-layouts: 18.4 us -> 2.9 us
    pallas_call x1, Pallas kernels: 177 us -> 156 us  [backward(): pl.pallas_call(functools.partial(backward_kernel, shards), out_shape=outs...]
    pallas_call x1, Pallas kernels: 121 us -> 110 us  [forward(): pl.pallas_call(functools.partial(forward_kernel, shards), out_shape=outs,...]
    unnamed x16 -> x0, local copies, waits for them, and re-layouts: 8.92 us -> none
    another operation x8 -> x0, local copies, waits for them, and re-layouts: 5.26 us -> none  [local(): jnp.stack(vectors)]
    pallas_call x0 -> x1, Pallas kernels: none -> 4.28 us  [place_results(): pl.pallas_call(functools.partial(place_kernel, n), out_shape=outs + (jax....]
where the time goes in v3:
time: 282 us; the launch traced here: 277 us
  Pallas kernels  271 us (96%)
  local copies, waits for them, and re-layouts  2.9 us (1%)
    pallas_call x1, Pallas kernels, backward(): pl.pallas_call(functools.partial(backward_kernel, shards), out_shape=outs...  156 us
    pallas_call x1, Pallas kernels, forward(): pl.pallas_call(functools.partial(forward_kernel, shards), out_shape=outs,...  110 us

profile of v3, /device:TPU:0, one launch (start us, length us, event | category | flops | bytes accessed | tf_op | source)
XLA Modules:
  0.0 277.0 jit_solution(1069196134859681064)
XLA Ops:
  1.4 0.7 broadcast_in_dim.79
  2.1 1.5 select_select_fusion.small_in
  3.5 0.7 broadcast_in_dim.70.live_in
  4.2 110.4 %shard_map.271 = (bf16[4,256,3072]{2,1,0:T(8,128)(2,1)}, bf16[4,256,1024]{2,1,0:T(8,128)(2,1)}, bf16[4,256,4096]{2,1,0:T(8,128)(2,1)}, bf16[4,1024,1024]{2,1,0:T...) custom-call(bf16[2,256,1024]{2,1,0:T(8,128)(2,1)} %bitcast.25, ...), custom_call_target="tpu_custom_call" | custom-call | tf_op jit(solution)/shard_map/pallas_call | solution.py:379
  114.6 156.2 %shard_map.272 = (bf16[2,256,1024]{2,1,0:T(8,128)(2,1)}, bf16[2,256,1024]{2,1,0:T(8,128)(2,1)}, bf16[64,3072]{1,0:T(8,128)(2,1)}, bf16[64,1024]{1,0:T(8,128)(2,1...) custom-call(bf16[2,256,1024]{2,1,0:T(8,128)(2,1)} %bitcast.26, ...), custom_call_target="tpu_custom_call" | custom-call | tf_op jit(solution)/shard_map/pallas_call | solution.py:866
  270.8 4.3 %shard_map.273 = (bf16[2,256,1024]{2,1,0:T(8,128)(2,1)}, bf16[2,256,1024]{2,1,0:T(8,128)(2,1)}, f32[64,3072]{1,0:T(8,128)}, f32[64,1024]{1,0:T(8,128)}, f32[64,4...) custom-call(bf16[2,256,1024]{2,1,0:T(8,128)(2,1)} %get-tuple-element.58.refs_0_, ...), custom_call_target="tpu_custom_call" | custom-call | tf_op jit(solution)/shard_map/pallas_call | solution.py:942
  275.1 1.5 slice_bitcast_fusion
  (7 shorter events, 0.0 us)

commit v4 on v3

--- a/solution.py
+++ b/solution.py
@@ -124,10 +124,10 @@
     x_moves = [net.move(x_in, xv.at[0])]
     x_sends = [net.send(x_in.at[0], xv.at[1, 0], place.to_y)]
 
-    chunks = [(wq_in, wq_all, part * width, 0, False) for part in (1, 2, 0)]
-    chunks.append((wo_in, wo_all, 0, 0, False))
-    chunks += [(wu_in, wu_all, j * width, 0, False) for j in range(hidden // width)]
-    chunks += [(wd_in, wd_all, 0, j * shard_rows, True) for j in range(wd_in.shape[0] // shard_rows)]
+    chunks = [(wq_in, wq_all.at[part], part * width, 0, False) for part in (1, 2, 0)]
+    chunks.append((wo_in, wo_all.at[0], 0, 0, False))
+    chunks += [(wu_in, wu_all.at[j], j * width, 0, False) for j in range(hidden // width)]
+    chunks += [(wd_in, wd_all.at[j], 0, j * shard_rows, True) for j in range(wd_in.shape[0] // shard_rows)]
     chunks = [chunk[:4] + (chunk[4] or i in IN_HALVES,) for i, chunk in enumerate(chunks)]
     state = [dict() for _ in chunks]
     others = pl.ds(1, shards - 1)
@@ -135,34 +135,32 @@
     near, far = {"shard": z + 1 - 2 * (z % 2)}, {"shard": z + 2 - 4 * (z // 2)}
     at_near = 1 + 2 * (z % 2)
 
-    def region(i, px, py, pc, side=None):
-        _, _, col, row, halves = chunks[i]
-        if halves:
-            h = (px + py) % 2
-            at, n = {None: (0, 2 * quarter), "x": (0, quarter), "y": (quarter, quarter)}[side]
-            rows = pl.ds(pl.multiple_of(row + pc * 2 * quarter + at, 16), n)
-            return rows, pl.ds(pl.multiple_of(col + h * (width // 2), 128), width // 2)
-        cut = width // 4
-        at, n = {None: (0, width), "y": (0, cut), "x": (cut, width - cut)}[side]
-        rows = pl.ds(pl.multiple_of(row + ((px * 2 + py) * 2 + pc) * eighth, 16), eighth)
-        return rows, pl.ds(col + at, n)
+    def region(i, px, py, pc, side=None, first=0):
+        if chunks[i][4]:
+            piece = ((px + py) % 2 * 2 + pc) * quarter
+            at, n = {None: (0, quarter), "x": (0, eighth), "y": (eighth, eighth)}[side]
+        else:
+            piece = ((px * 2 + py) * 2 + pc) * eighth
+            at, n = {None: (0, eighth), "y": (0, eighth // 2), "x": (eighth // 2, eighth // 2)}[side]
+        return pl.ds(pl.multiple_of(first + piece + at, 16), n)
 
     def start_z(i):
-        src, all_, *_ = chunks[i]
-        at = region(i, x, y, c)
-        state[i]["far"] = net.send(src.at[at], all_.at[(2,) + at], far)
-        state[i]["near"] = net.send(src.at[at], all_.at[(at_near,) + at], near)
+        src, all_, col, row, _ = chunks[i]
+        rows = region(i, x, y, c)
+        src = src.at[region(i, x, y, c, None, row), pl.ds(col, width)]
+        state[i]["far"] = net.send(src, all_.at[2, rows], far)
+        state[i]["near"] = net.send(src, all_.at[at_near, rows], near)
 
     def relay(i):
         all_ = chunks[i][1]
-        at = region(i, x, y, c)
+        rows = region(i, x, y, c)
         state[i]["far"].wait_recv()
-        state[i]["relay"] = net.send(all_.at[(2,) + at], all_.at[(4 - at_near,) + at], near)
+        state[i]["relay"] = net.send(all_.at[2, rows], all_.at[4 - at_near, rows], near)
         if i + AHEAD < len(chunks):
             start_z(i + AHEAD)
 
     def pass_piece(i, px, py, pc, peer, side=None):
-        ref = chunks[i][1].at[(others,) + region(i, px, py, pc, side)]
+        ref = chunks[i][1].at[others, region(i, px, py, pc, side)]
         return net.send(ref, ref, peer)
 
     def plane_one(i):
@@ -204,7 +202,7 @@
         for s in range(shards):
             rows = pl.ds(pl.multiple_of(place.behind(s) * shard_rows, shard_rows), shard_rows)
             cs = pl.ds(col, width)
-            from_ = src.at[:, cs] if s == 0 else all_.at[s, :, cs]
+            from_ = src.at[:, cs] if s == 0 else all_.at[s]
             moves.append(net.move(from_, dst.at[rows, cs]))
         return moves
 
@@ -370,8 +368,9 @@
     pairs = width // PAIR
     any_ = pl.BlockSpec(memory_space=pl.ANY)
     sd = jax.ShapeDtypeStruct
+    square = (shards, wq.shape[0], width)
     outs = (
-        sd((shards,) + wq.shape, BF), sd((shards,) + wo.shape, BF), sd((shards,) + wu.shape, BF), sd((shards,) + wd.shape, BF),
+        sd((3,) + square, BF), sd((1,) + square, BF), sd((hidden // width,) + square, BF), sd((wd.shape[0] // wq.shape[0],) + square, BF),
         sd((2, tokens, width), BF), sd((tokens, width), BF), sd((slots, 2, 4, length, width), BF),
         sd((slots, pairs, 1, 2 * length), F32), sd((tokens, width), BF), sd((tokens, width), F32),
         sd((tokens, width), BF), sd((tokens, hidden), BF), sd((tokens, hidden), BF), sd((shards,) + small.shape, BF),
@@ -407,6 +406,7 @@
 N_REMOTE2, N_LOCAL2 = 160, 80
 RING_A, RING_B, N_CHUNKS = 3, 3, 12
 X_ONLY = (8, 9)
+IN_PARTS = (11,)
 
 
 def norm_back(values, gain, incoming):
@@ -450,16 +450,21 @@
     cot_moves = [net.move(cot_in.at[slot], dm.at[span(slot)]) for slot in range(slots)]
     act_moves = [net.move(act_in, ad.at[0])]
 
-    def blocks_of(own, gathered, cols, dst_of):
+    def blocks_of(own, gathered, dst_of):
         moves = []
         for s in range(shards):
-            src = own.at[:, cols] if s == 0 else gathered.at[s, :, cols]
-            moves.append(net.move(src, dst_of(place.behind(s))))
+            dst = dst_of(place.behind(s))
+            if s == 0:
+                moves.append(net.move(own, dst))
+                continue
+            for j, square in enumerate(gathered):
+                at = (pl.ds(j * shard_rows, shard_rows),) if own.shape[0] > shard_rows else (slice(None), pl.ds(j * width, width))
+                moves.append(net.move(square.at[s], dst.at[at]))
         return moves
 
-    every = pl.ds(0, width)
     wd_moves = blocks_of(
-        wd_in, wd_all, every, lambda a: wa.at[pl.ds(pl.multiple_of(a * down_rows, down_rows), down_rows)]
+        wd_in, [wd_all.at[j] for j in range(down_rows // shard_rows)],
+        lambda a: wa.at[pl.ds(pl.multiple_of(a * down_rows, down_rows), down_rows)],
     )
     place.greet()
 
@@ -468,7 +473,6 @@
         dm[span(slot)] = dm[span(slot)] * live_in[slot].astype(BF)
     net.wait(act_moves)
 
-    chunks = []
     flights = []
 
     def first_peer(k, p):
@@ -477,118 +481,141 @@
     def credit(k, p):
         return free_sems.at[2 if p else 3 if k in X_ONLY else 1]
 
-    def advance_zero(k):
-        st, a, b = chunks[k], k % RING_A, k % RING_B
+    def advance_zero(st):
+        k, rows = st["k"], st["rows"]
+        a, b = k % RING_A, k % RING_B
         st["s0"].wait_recv()
 
         @pl.loop(0, 4)
         def _(i):
-            gbuf[a, c, i] = gbuf[a, c, i] + r0[a, i]
-
-        pl.semaphore_signal(free_sems.at[0], inc=1, device_id=place.to_c, device_id_type=MESH)
+            gbuf[a, c, i, :, :, rows, :] = gbuf[a, c, i, :, :, rows, :] + r0[a, i, :, :, rows, :]
+
+        if st["last"]:
+            pl.semaphore_signal(free_sems.at[0], inc=1, device_id=place.to_c, device_id_type=MESH)
         st["s1"] = []
         for p in range(2):
-            if k >= RING_B:
+            if k >= RING_B and st["first"]:
                 pl.semaphore_wait(credit(k, p), 1)
             peer = first_peer(k, p)
-            src = gbuf.at[a, c, 2 * p + 1 - x] if peer is place.to_x else gbuf.at[a, c, pl.ds(2 * p, 2), 1 - y]
-            st["s1"].append(net.send(src, r1.at[b, p], peer))
-
-    def advance_one(k):
-        st, a, b = chunks[k], k % RING_A, k % RING_B
+            if peer is place.to_x:
+                src = gbuf.at[a, c, 2 * p + 1 - x, :, :, rows, :]
+            else:
+                src = gbuf.at[a, c, pl.ds(2 * p, 2), 1 - y, :, rows, :]
+            st["s1"].append(net.send(src, r1.at[b, p, :, :, rows, :], peer))
+
+    def advance_one(st):
+        k, rows = st["k"], st["rows"]
+        a, b = k % RING_A, k % RING_B
         for p in range(2):
             st["s1"][p].wait_recv()
             for i in range(2):
-                kept = gbuf[a, c, 2 * p + x, i] if first_peer(k, p) is place.to_x else gbuf[a, c, 2 * p + i, y]
-                value = kept + r1[b, p, i]
+                if first_peer(k, p) is place.to_x:
+                    kept = gbuf[a, c, 2 * p + x, i, :, rows, :]
+                else:
+                    kept = gbuf[a, c, 2 * p + i, y, :, rows, :]
+                value = kept + r1[b, p, i, :, rows, :]
                 for zz in range(shards):
-                    fbuf[b, zz % 2, zz // 2, 2 * p + i] = value[zz]
+                    fbuf[b, zz % 2, zz // 2, 2 * p + i, rows, :] = value[zz]
             if k + RING_B < N_CHUNKS:
                 peer = first_peer(k + RING_B, p)
                 pl.semaphore_signal(credit(k + RING_B, p), inc=1, device_id=peer, device_id_type=MESH)
-        st["sa"] = net.send(fbuf.at[b, 1 - z % 2], ra.at[k], {"shard": z + 1 - 2 * (z % 2)})
+        near = {"shard": z + 1 - 2 * (z % 2)}
+        st["sa"] = net.send(fbuf.at[b, 1 - z % 2, :, :, rows, :], ra.at[k, :, :, rows, :], near)
         for copy in [st["s0"]] + st["s1"]:
             copy.wait_send()
 
-    def advance_two(k):
-        st, b = chunks[k], k % RING_B
+    def advance_two(st):
+        k, rows = st["k"], st["rows"]
+        b = k % RING_B
         st["sa"].wait_recv()
         for i in range(2):
-            gb[b, i] = fbuf[b, z % 2, i] + ra[k, i]
-        st["sb"] = net.send(gb.at[b, 1 - z // 2], rb.at[k], {"shard": z + 2 - 4 * (z // 2)})
+            gb[b, i, :, rows, :] = fbuf[b, z % 2, i, :, rows, :] + ra[k, i, :, rows, :]
+        far = {"shard": z + 2 - 4 * (z // 2)}
+        st["sb"] = net.send(gb.at[b, 1 - z // 2, :, rows, :], rb.at[k, :, rows, :], far)
         st["sa"].wait_send()
 
-    def advance_three(k):
-        st, b = chunks[k], k % RING_B
+    def advance_three(st):
+        k, rows = st["k"], st["rows"]
+        b = k % RING_B
         st["sb"].wait_recv()
-        tsum[b] = gb[b, z // 2] + rb[k]
+        tsum[b, :, rows, :] = gb[b, z // 2, :, rows, :] + rb[k, :, rows, :]
         st["s2"] = []
         for p in range(2):
             over_y = first_peer(k, p) is place.to_x
-            src = tsum.at[b, 2 * p + 1 - (y if over_y else x)]
-            st["s2"].append(net.send(src, r2.at[k, p], place.to_y if over_y else place.to_x))
+            src = tsum.at[b, 2 * p + 1 - (y if over_y else x), rows, :]
+            st["s2"].append(net.send(src, r2.at[k, p, rows, :], place.to_y if over_y else place.to_x))
         st["sb"].wait_send()
 
-    def advance_four(k):
-        st, b = chunks[k], k % RING_B
+    def advance_four(st):
+        k, rows = st["k"], st["rows"]
+        b = k % RING_B
         for p in range(2):
             st["s2"][p].wait_recv()
             at = y if first_peer(k, p) is place.to_x else x
-            tbuf[b, p] = tsum[b, 2 * p + at] + r2[k, p]
-        st["s4"] = net.send(tbuf.at[b], r4.at[k], place.to_x)
+            tbuf[b, p, rows, :] = tsum[b, 2 * p + at, rows, :] + r2[k, p, rows, :]
+        st["s4"] = net.send(tbuf.at[b, :, rows, :], r4.at[k, :, rows, :], place.to_x)
         for copy in st["s2"]:
             copy.wait_send()
 
-    def advance_five(k):
-        st, b = chunks[k], k % RING_B
+    def advance_five(st):
+        k, rows = st["k"], st["rows"]
+        b = k % RING_B
         st["s4"].wait_recv()
         out, kind, col = st["out"]
         for source, slot, at in ((tbuf, b, x), (r4, k, 1 - x)):
             for p in range(2):
-                value = source[slot, p]
+                value = source[slot, p, rows, :]
                 if kind == "cols":
-                    lanes = pl.ds(pl.multiple_of(col + p * 2 * block + at * block, block), block)
-                    out[:, lanes] = value
+                    out[rows, pl.ds(pl.multiple_of(col + p * 2 * block + at * block, block), block)] = value
                 else:
-                    rows = pl.ds(pl.multiple_of((p * 2 + at) * 64, 64), 64)
-                    out[rows, pl.ds(col, block)] = value
+                    out[pl.ds(pl.multiple_of((p * 2 + at) * 64 + rows.start, 16), rows.size), pl.ds(col, block)] = value
         st["s4"].wait_send()
 
     stages = (advance_zero, advance_one, advance_two, advance_three, advance_four, advance_five)
 
     def pump():
-        for flight in reversed(flights):
-            if flight[1] < len(stages):
-                stages[flight[1]](flight[0])
-                flight[1] += 1
+        for st in reversed(flights):
+            if st["stage"] < len(stages):
+                stages[st["stage"]](st)
+                st["stage"] += 1
+
+    def next_chunk():
+        return flights[-1]["k"] + 1 if flights else 0
 
     def launch(out, kind, col):
-        k = len(chunks)
+        k = next_chunk()
         a = k % RING_A
         if k >= RING_A:
             pl.semaphore_wait(free_sems.at[0], 1)
-        chunks.append({"out": (out, kind, col)})
-        chunks[k]["s0"] = net.send(gbuf.at[a, 1 - c], r0.at[a], place.to_c)
-        flights.append([k, 0])
+        parts = 2 if k in IN_PARTS else 1
+        made = []
+        for part in range(parts):
+            rows = pl.ds(part * (64 // parts), 64 // parts)
+            st = {"k": k, "stage": 0, "rows": rows, "out": (out, kind, col)}
+            st["first"], st["last"] = part == 0, part == parts - 1
+            st["s0"] = net.send(gbuf.at[a, 1 - c, :, :, :, rows, :], r0.at[a, :, :, :, rows, :], place.to_c)
+            made.append(st)
+        flights.extend(reversed(made))
 
     def grad_cols(pairs, out, col):
-        a = len(chunks) % RING_A
-
-        @pl.loop(0, 4)
+        a = next_chunk() % RING_A
+
+        @pl.loop(0, 2)
         def _(i):
             total = None
             for left, right in pairs:
                 term = dot(left[...], right(i), TN)
                 total = term if total is None else total + term
-            value = total.astype(BF).reshape(shards, 2, 2, 64, block)
-            for cc in range(2):
-                for yy in range(2):
-                    gbuf[a, cc, i, yy] = value[:, yy, cc]
+            for j in range(2):
+                value = total[:, j * block : (j + 1) * block].astype(BF).reshape(shards, 2, 2, 64, block)
+                for cc in range(2):
+                    for yy in range(2):
+                        gbuf[a, cc, i * 2 + j, yy] = value[:, yy, cc]
 
         launch(out, "cols", col)
 
     def grad_down(j):
-        a = len(chunks) % RING_A
+        a = next_chunk() % RING_A
         right = dm[:, pl.ds(j * block, block)]
 
         @pl.loop(0, shards)
@@ -609,12 +636,12 @@
     half_rows = width // 2
     per = half_rows // shard_rows
     wu_moves = blocks_of(
-        wu_in, wu_all, pl.ds(0, hidden),
+        wu_in, [wu_all.at[j] for j in range(hidden // width)],
         lambda a: wb.at[a // per, pl.ds(pl.multiple_of((a % per) * shard_rows, shard_rows), shard_rows)],
     )
     nm_moves = [net.move(res_in, res), net.move(nm_in, nm)]
     wo_moves = blocks_of(
-        wo_in, wo_all, every,
+        wo_in, [wo_all.at[0]],
         lambda a: normed.at[a // per, pl.ds(pl.multiple_of((a % per) * shard_rows, shard_rows), shard_rows)],
     )
     late_moves = [net.move(att_in, att), net.move(q_in, qv), net.move(lse_in, lsev)]
@@ -674,7 +701,7 @@
     pl.semaphore_signal(act_free, inc=1, device_id=place.to_c, device_id_type=MESH)
 
     def up_pairs(j):
-        return [(nm, lambda i: ad[1, :, lanes_at(j * width + i * block)])]
+        return [(nm, lambda i: ad[1, :, lanes_at(j * width + i * 2 * block, 2 * block)])]
 
     pump()
     grad_cols(up_pairs(0), gu, 0)
@@ -741,12 +768,12 @@
     for part in (1, 2, 0):
         wq_moves.append(
             blocks_of(
-                wq_in, wq_all, pl.ds(part * width, width),
+                wq_in.at[:, pl.ds(part * width, width)], [wq_all.at[part]],
                 lambda a: wa.at[pl.ds(pl.multiple_of(part * width + a * shard_rows, shard_rows), shard_rows)],
             )
         )
     pump()
-    grad_cols([(att, lambda i: dbr[:, lanes_at(i * block)])], go, 0)
+    grad_cols([(att, lambda i: dbr[:, lanes_at(i * 2 * block, 2 * block)])], go, 0)
     sg[2:3] = col_sum(qv[...])
 
     for slot in range(slots):
@@ -769,13 +796,13 @@
     back_sends = [net.send(dm.at[span(slot)], dn.at[slot], place.to_y) for slot in range(slots)]
     pump()
     net.wait(normed_moves)
-    grad_cols([(normed.at[0], lambda i: qv[:, lanes_at(i * block)])], gq, 0)
+    grad_cols([(normed.at[0], lambda i: qv[:, lanes_at(i * 2 * block, 2 * block)])], gq, 0)
     sg[3:4] = col_sum(d_part(1, 0)) + col_sum(d_part(1, 1))
     pump()
 
     def kv_pairs(part):
         return [
-            (normed.at[which], lambda i, which=which: d_part(part, which, i * block, block)) for which in range(2)
+            (normed.at[which], lambda i, which=which: d_part(part, which, i * 2 * block, 2 * block)) for which in range(2)
         ]
 
     grad_cols(kv_pairs(0), gq, width)
@@ -828,19 +855,19 @@
     sums[-1].wait_recv()
     sr[3] = sr[6] + sr[2]
     out_moves.append(net.move(sr.at[3], sg_out))
-    while any(flight[1] < len(stages) for flight in flights):
+    while any(st["stage"] < len(stages) for st in flights):
         pump()
     for _ in range(RING_A):
         pl.semaphore_wait(free_sems.at[0], 1)
     out_moves += [net.move(a, b) for a, b in ((gq, gq_out), (go, go_out), (gu, gu_out), (gd, gd_out))]
-    finish(net, chunks)
-
-
-def finish(net, chunks):
+    finish(net, flights)
+
+
+def finish(net, flights):
     done = set()
-    for st in chunks:
+    for st in flights:
         for name, value in st.items():
-            if name.startswith("s"):
+            if name in ("s0", "s1", "sa", "sb", "s2", "s4"):
                 done.update(id(copy) for copy in (value if isinstance(value, list) else [value]))
     for copy in net.remote:
         if id(copy) not in done:

time: 282 us -> 280 us (level)
    pallas_call x1, Pallas kernels: 156 us -> 153 us  [backward(): pl.pallas_call(functools.partial(backward_kernel, shards), out_shape=outs...]
where the time goes in v4:
time: 280 us; the launch traced here: 275 us
  Pallas kernels  269 us (96%)
  local copies, waits for them, and re-layouts  2.9 us (1%)
    pallas_call x1, Pallas kernels, backward(): pl.pallas_call(functools.partial(backward_kernel, shards), out_shape=outs...  153 us
    pallas_call x1, Pallas kernels, forward(): pl.pallas_call(functools.partial(forward_kernel, shards), out_shape=outs,...  111 us

profile of v4, /device:TPU:0, one launch (start us, length us, event | category | flops | bytes accessed | tf_op | source)
XLA Modules:
  0.0 274.7 jit_solution(1591725750981235397)
XLA Ops:
  1.4 0.7 broadcast_in_dim.79
  2.1 1.5 select_select_fusion.small_in
  3.5 0.7 broadcast_in_dim.70.live_in
  4.2 111.2 %shard_map.271 = (bf16[3,4,256,1024]{3,2,1,0:T(8,128)(2,1)}, bf16[1,4,256,1024]{3,2,1,0:T(8,128)(2,1)}, bf16[4,4,256,1024]{3,2,1,0:T(8,128)(2,1)}, bf16[4,4,256,...) custom-call(bf16[2,256,1024]{2,1,0:T(8,128)(2,1)} %bitcast.25, ...), custom_call_target="tpu_custom_call" | custom-call | tf_op jit(solution)/shard_map/pallas_call | solution.py:378
  115.4 153.1 %shard_map.272 = (bf16[2,256,1024]{2,1,0:T(8,128)(2,1)}, bf16[2,256,1024]{2,1,0:T(8,128)(2,1)}, bf16[64,3072]{1,0:T(8,128)(2,1)}, bf16[64,1024]{1,0:T(8,128)(2,1...) custom-call(bf16[2,256,1024]{2,1,0:T(8,128)(2,1)} %bitcast.26, ...), custom_call_target="tpu_custom_call" | custom-call | tf_op jit(solution)/shard_map/pallas_call | solution.py:893
  268.5 4.3 %shard_map.273 = (bf16[2,256,1024]{2,1,0:T(8,128)(2,1)}, bf16[2,256,1024]{2,1,0:T(8,128)(2,1)}, f32[64,3072]{1,0:T(8,128)}, f32[64,1024]{1,0:T(8,128)}, f32[64,4...) custom-call(bf16[2,256,1024]{2,1,0:T(8,128)(2,1)} %get-tuple-element.58.refs_0_, ...), custom_call_target="tpu_custom_call" | custom-call | tf_op jit(solution)/shard_map/pallas_call | solution.py:969
  272.8 1.5 slice_bitcast_fusion
  (7 shorter events, 0.0 us)

commit v5 on v4

--- a/solution.py
+++ b/solution.py
@@ -425,7 +425,7 @@
 
 def backward_kernel(
     shards,
-    x_in, cot_in, live_in, small_in, wq_in, wo_in, wu_in, wd_in, wq_all, wo_all, wu_all, wd_all,
+    x_in, cot_in, small_in, wq_in, wo_in, wu_in, wd_in, wq_all, wo_all, wu_all, wd_all,
     normed_in, q_in, kv_in, lse_in, att_in, res_in, nm_in, act_in, slope_in,
     layer_out, input_out, gq_out, go_out, gu_out, gd_out, sg_out,
     wa, wb, ad, nm, att, res, dm, dbr, qv, normed, xv, dn, lsev,
@@ -468,9 +468,12 @@
     )
     place.greet()
 
+    def live(slot):
+        return jnp.concatenate([small_in[z, 12 + slot : 13 + slot]] * shards, axis=1)
+
     net.wait(cot_moves)
     for slot in range(slots):
-        dm[span(slot)] = dm[span(slot)] * live_in[slot].astype(BF)
+        dm[span(slot)] = dm[span(slot)] * live(slot)
     net.wait(act_moves)
 
     flights = []
@@ -676,7 +679,7 @@
     for slot in range(slots):
         rows = span(slot)
         value = res[rows] + dot(ad[0, rows], wa[...]) + down_bias
-        xv[slot] = (value * live_in[slot]).astype(BF)
+        xv[slot] = (value * live(slot).astype(F32)).astype(BF)
         incoming = jnp.concatenate([dot(ad[1, rows], wb[i], NT) for i in range(2)], axis=1)
         back, terms = norm_back(res[rows], gain, incoming)
         back = back + dm[rows].astype(F32)
@@ -875,7 +878,7 @@
     net.wait(net.local)
 
 
-def backward(shards, x, cot, live, small, weights, gathered, kept):
+def backward(shards, x, cot, small, weights, gathered, kept):
     slots, length, width = x.shape
     tokens = slots * length
     hidden = weights[2].shape[1]
@@ -893,7 +896,7 @@
     return pl.pallas_call(
         functools.partial(backward_kernel, shards),
         out_shape=outs,
-        in_specs=[any_] * 2 + [vmem] * 2 + [any_] * 17,
+        in_specs=[any_] * 2 + [vmem] + [any_] * 17,
         out_specs=(any_,) * len(outs),
         scratch_shapes=[
             pltpu.VMEM((hidden, width), BF),
@@ -934,7 +937,7 @@
             pltpu.SemaphoreType.REGULAR,
         ],
         compiler_params=pltpu.CompilerParams(collective_id=2, has_side_effects=True, vmem_limit_bytes=63 * MIB),
-    )(x, cot, live, small, *weights, *gathered, *kept)
+    )(x, cot, small, *weights, *gathered, *kept)
 
 
 def place_kernel(n, *refs):
@@ -988,16 +991,15 @@
     slots, length, width = x.shape
     rows = w_qkv.shape[0]
     vectors = [attn_gain, attn_shift, q_bias, v_bias, out_bias, mlp_gain, mlp_shift, down_bias]
-    small = jnp.broadcast_to(up_bias.reshape(1, 4, rows), (4, 4, rows)).reshape(16, rows)
+    vectors += [up_bias[i * rows : (i + 1) * rows] for i in range(4)]
     row = lax.broadcasted_iota(jnp.int32, (16, rows), 0)
+    small = (row - len(vectors) < clip_loads[0]).astype(BF)
     for i, vector in enumerate(vectors):
         small = jnp.where(row == i, vector[None, :], small)
     weights = (w_qkv, w_out, w_up, w_down)
     *gathered, normed, q, kv, lse, att, res, nm, act, slope, small = forward(shards, x, small, *weights)
-    live = (jnp.arange(slots) < clip_loads[0]).astype(F32)
-    live = jnp.broadcast_to(live[:, None, None], (slots, 1, width))
     kept = (normed, q, kv.reshape(-1, width), lse, att, res, nm, act, slope)
-    layer_out, input_grad, gq, go, gu, gd, sums = backward(shards, x, cot, live, small, weights, gathered, kept)
+    layer_out, input_grad, gq, go, gu, gd, sums = backward(shards, x, cot, small, weights, gathered, kept)
     pods = lax.axis_size("replica")
     if pods > 2:
         ends = [[p for p in range(pods) if p % 2 == side] for side in range(2)]

time: 280 us -> 279 us (level)
  no operation moved by 1% of the time
where the time goes in v5:
time: 279 us; the launch traced here: 274 us
  Pallas kernels  269 us (96%)
    pallas_call x1, Pallas kernels, backward(): pl.pallas_call(functools.partial(backward_kernel, shards), out_shape=outs...  153 us
    pallas_call x1, Pallas kernels, forward(): pl.pallas_call(functools.partial(forward_kernel, shards), out_shape=outs,...  111 us

profile of v5, /device:TPU:0, one launch (start us, length us, event | category | flops | bytes accessed | tf_op | source)
XLA Modules:
  0.0 274.2 jit_solution(4253574669923728431)
XLA Ops:
  1.4 0.8 fusion
  2.2 1.5 select_select_fusion.small_in
  3.7 111.1 %shard_map.271 = (bf16[3,4,256,1024]{3,2,1,0:T(8,128)(2,1)}, bf16[1,4,256,1024]{3,2,1,0:T(8,128)(2,1)}, bf16[4,4,256,1024]{3,2,1,0:T(8,128)(2,1)}, bf16[4,4,256,...) custom-call(bf16[2,256,1024]{2,1,0:T(8,128)(2,1)} %bitcast.25, ...), custom_call_target="tpu_custom_call" | custom-call | tf_op jit(solution)/shard_map/pallas_call | solution.py:378
  114.8 153.1 %shard_map.272 = (bf16[2,256,1024]{2,1,0:T(8,128)(2,1)}, bf16[2,256,1024]{2,1,0:T(8,128)(2,1)}, bf16[64,3072]{1,0:T(8,128)(2,1)}, bf16[64,1024]{1,0:T(8,128)(2,1...) custom-call(bf16[2,256,1024]{2,1,0:T(8,128)(2,1)} %bitcast.26, ...), custom_call_target="tpu_custom_call" | custom-call | tf_op jit(solution)/shard_map/pallas_call | solution.py:896
  268.0 4.3 %shard_map.273 = (bf16[2,256,1024]{2,1,0:T(8,128)(2,1)}, bf16[2,256,1024]{2,1,0:T(8,128)(2,1)}, f32[64,3072]{1,0:T(8,128)}, f32[64,1024]{1,0:T(8,128)}, f32[64,4...) custom-call(bf16[2,256,1024]{2,1,0:T(8,128)(2,1)} %get-tuple-element.58.refs_0_, ...), custom_call_target="tpu_custom_call" | custom-call | tf_op jit(solution)/shard_map/pallas_call | solution.py:972
  272.3 1.5 slice_bitcast_fusion
  (7 shorter events, 0.0 us)
